TPU v7x, 32 devices: a whole 2x2x4 slice. The times are simulated.
32 devices in a mesh: groups: 2 (over x), cells: 16 (over z, y, core).
Axes of the slice: x: 2, y: 2, z: 4, core: 2. Of those that a mesh axis runs over, the one named last changes fastest.
Arguments:
- probes: float32 [8, 16, 128, 512], P('groups', None, 'cells'), parts along dimension 0, may hold values from -6 to 6
- wind_field: float32 [3, 16, 128, 512], P(None, None, 'cells'), may hold values from -1 to 1
- prior_scale: float32 [16, 128, 512], P(None, 'cells'), may hold values from 0.5 to 3
- eigen_basis: float32 [128, 512, 128], P('cells'), may hold values from -0.0234375 to 0.0234375
- eigen_values: float32 [128], replicated, may hold values from 0.1 to 100
- kernel_rows: float32 [512, 512], P(('groups', 'cells')), parts along dimension 0, may hold values from 0.2 to 1
- obs_weight: float32 [512, 32], P(('groups', 'cells')), parts along dimension 0, may hold values from 0.3 to 3
- tile_column: int32 [512, 32], P(('groups', 'cells')), parts along dimension 0, may hold values from -1 to 4095, as said below
Outputs:
- hessian_probes: float32 [8, 16, 128, 512], P('groups', None, 'cells'), parts along dimension 0
- misfit: float32 [512, 128], P(('groups', 'cells')), parts along dimension 0
- coeffs: float32 [8, 128], P('groups'), parts along dimension 0
There are 2 independent parts, one for each index of `groups`. A program takes and returns all parts, laid end to end along the dimension named above; an argument that names none is the same for every part. Nothing has to cross between parts.
Inputs may be any that keep to these rules, and one draw needn't show every extreme that they name: `tile_column`: -1 marks an empty slot; the live slots of a row come first; in every draw some tiles receive 32 live slots from every tile.
All inputs are finite; a program needn't handle non-finite values.
Results may differ from a plain program's by a relative error of at most 0.00013.
Values sent between devices are 32-bit elements; how exact they have to be, the bound alone decides.
A program may use at most 128 MiB of HBM per device.

v0:
```python
import jax
import jax.numpy as jnp
from jax import lax
from jax.sharding import PartitionSpec as P

LEV = 16
STEPS = 4
CAP = 32


def shifted(value, axis, by):
    devices = lax.axis_size(axis)
    return lax.ppermute(value, axis, [(i, (i + by) % devices) for i in range(devices)])


def padded(block, sides, width):
    for axis, dim in sides:
        count = lax.axis_size(axis)
        forward = [(i, i + 1) for i in range(count - 1)]
        forward.append((count - 1, 0))
        backward = [(target, source) for source, target in forward]
        low = lax.ppermute(
            lax.slice_in_dim(block, block.shape[dim] - width, None, axis=dim), axis, forward
        )
        high = lax.ppermute(lax.slice_in_dim(block, 0, width, axis=dim), axis, backward)
        block = jnp.concatenate([low, block, high], axis=dim)
    return block


def courants(wind_field):
    return (0.3 * wind_field[0], 0.15 * wind_field[1], 0.025 * (1.0 + wind_field[2]))


def vertical_mixing(center, mixing):
    upward = mixing[1:] * (center[:, :-1] - center[:, 1:])
    nothing = jnp.zeros_like(upward[:, :1])
    return jnp.concatenate([nothing, upward], axis=1) - jnp.concatenate([upward, nothing], axis=1)


def forward_step(tracer, wind_field):
    east_rate, north_rate, mixing = courants(wind_field)
    east_pos = jnp.maximum(east_rate, 0.0)
    east_neg = jnp.minimum(east_rate, 0.0)
    west_flux = east_pos[:, 1:] * tracer[:, :, :-1] + east_neg[:, 1:] * tracer[:, :, 1:]
    center = tracer[:, :, 1:-1]
    result = center - (west_flux[:, :, 1:] - west_flux[:, :, :-1])
    north_pos = jnp.maximum(north_rate[:, 1:-1], 0.0)
    north_neg = jnp.minimum(north_rate[:, 1:-1], 0.0)
    south_flux = north_pos[..., 1:] * center[..., :-1] + north_neg[..., 1:] * center[..., 1:]
    nothing = jnp.zeros_like(south_flux[..., :1])
    all_faces = jnp.concatenate([nothing, south_flux, nothing], axis=-1)
    result = result - (all_faces[..., 1:] - all_faces[..., :-1])
    return result + vertical_mixing(center, mixing[:, 1:-1])


def backward_step(adjoint, wind_field):
    east_rate, north_rate, mixing = courants(wind_field)
    east_pos = jnp.maximum(east_rate, 0.0)
    east_neg = jnp.minimum(east_rate, 0.0)
    east_diff = adjoint[:, :, 1:] - adjoint[:, :, :-1]
    center = adjoint[:, :, 1:-1]
    result = (
        center + east_pos[:, 2:] * east_diff[:, :, 1:] + east_neg[:, 1:-1] * east_diff[:, :, :-1]
    )
    north_pos = jnp.maximum(north_rate[:, 1:-1], 0.0)
    north_neg = jnp.minimum(north_rate[:, 1:-1], 0.0)
    lat_diff = center[..., 1:] - center[..., :-1]
    upper_part = north_pos[..., 1:] * lat_diff
    lower_part = north_neg[..., 1:] * lat_diff
    nothing = jnp.zeros_like(lat_diff[..., :1])
    result = (
        result
        + jnp.concatenate([upper_part, nothing], axis=-1)
        + jnp.concatenate([nothing, lower_part], axis=-1)
    )
    return result + vertical_mixing(center, mixing[:, 1:-1])


def local(
    probes, wind_field, prior_scale, eigen_basis, eigen_values, kernel_rows, obs_weight, tile_column
):
    probe_count = probes.shape[0]
    lon_width = probes.shape[2]
    lat_rows = probes.shape[3]
    tile_count = kernel_rows.shape[0]
    cells_tile = lon_width * lat_rows
    slot_count = tile_count * CAP
    kernel_recv = lax.all_to_all(kernel_rows, "cells", split_axis=0, concat_axis=0, tiled=True)
    east_column = shifted(wind_field[:, :, :1], "cells", -1)
    wind_ext = jnp.concatenate([jnp.zeros_like(east_column), wind_field, east_column], axis=2)
    tracer = prior_scale[None] * probes
    for section_index in range(STEPS):
        extended = padded(tracer, (("cells", 2),), 1)
        tracer = forward_step(extended, wind_ext)
    flat_tracer = tracer.reshape(probe_count, LEV, cells_tile)
    column_list = tile_column.reshape(-1)
    present = column_list >= 0
    present_f = present.astype(jnp.float32)
    safe_column = jnp.maximum(column_list, 0)
    sampled = jnp.take(flat_tracer, safe_column, axis=2)
    kernel_slots = (
        kernel_recv.reshape(tile_count, LEV, CAP).transpose(1, 0, 2).reshape(LEV, slot_count)
    )
    modeled = jnp.sum(kernel_slots[None] * sampled, axis=1) * present_f
    arrived = lax.all_to_all(
        modeled.reshape(probe_count, tile_count, CAP)
        .transpose(1, 0, 2)
        .reshape(tile_count, probe_count * CAP),
        "cells",
        split_axis=0,
        concat_axis=0,
        tiled=True,
    )
    misfit = (arrived.reshape(tile_count, probe_count, CAP) * obs_weight[:, None, :]).reshape(
        tile_count, probe_count * CAP
    )
    weighted = (
        lax.all_to_all(misfit, "cells", split_axis=0, concat_axis=0, tiled=True)
        .reshape(tile_count, probe_count, CAP)
        .transpose(1, 0, 2)
        .reshape(probe_count, slot_count)
    )
    contrib = kernel_slots[None] * weighted[:, None] * present_f
    stacked = contrib.transpose(2, 0, 1)
    segment_ids = jnp.where(present, column_list, cells_tile)
    summed = jax.ops.segment_sum(stacked, segment_ids, num_segments=cells_tile + 1)[:cells_tile]
    adjoint = summed.reshape(lon_width, lat_rows, probe_count, LEV).transpose(2, 3, 0, 1)
    for section_index in range(STEPS):
        extended = padded(adjoint, (("cells", 2),), 1)
        adjoint = backward_step(extended, wind_ext)
    hessian_probes = probes + prior_scale[None] * adjoint
    partial_sums = jnp.einsum(
        "kxy,xyr->kr", hessian_probes[:, 0], eigen_basis, precision=lax.Precision.HIGHEST
    )
    projection = lax.psum(partial_sums, "cells")
    coeffs = eigen_values / (1.0 + eigen_values) * projection
    return (hessian_probes, misfit, coeffs)


def solution(mesh):
    in_specs = (
        P("groups", None, "cells", None),
        P(None, None, "cells", None),
        P(None, "cells", None),
        P("cells", None, None),
        P(),
        P(("groups", "cells"), None),
        P(("groups", "cells"), None),
        P(("groups", "cells"), None),
    )
    out_specs = (P("groups", None, "cells", None), P(("groups", "cells"), None), P("groups", None))
    return jax.shard_map(local, mesh=mesh, in_specs=in_specs, out_specs=out_specs, check_vma=False)
```

profile of v0, /device:TPU:0, one launch (start us, length us, event | category | flops | bytes accessed | tf_op | source)
XLA Modules:
  0.0 260.6 jit_solution(8576446735294617085)
XLA Ops:
  0.6 1.5 all_to_all.18
  2.2 7.4 %all-to-all-start = ((f32[16,1,512]{2,1,0:T(1,128)}), f32[16,1,512]{2,1,0:T(1,128)S(1)}, u32[]{:S(2)}, u32[]{:S(2)}) async-start(f32[16,1,512]{2,1,0:T(1,128)} %all_to_all.18), calls=%async_computation | async-start | bytes 65536 | tf_op jit(solution)/shard_map/all_to_all | solution.py:88
  9.6 1.2 slice.360
  10.8 4.4 %collective-permute-start = (f32[3,16,1,512]{3,1,2,0:T(8,128)S(1)}, f32[3,16,1,512]{3,1,2,0:T(8,128)}, u32[]{:S(2)}, u32[]{:S(2)}) collective-permute-start(f32[3,16,1,512]{3,1,2,0:T(8,128)S(1)} %copy.59), channel_id=1, source_target_pairs={{0,15},{1,0},{2,1},{3,2},{4,3},{5,4},{6,5},{7,6},{8,7},{9,8},{10,9... | collective-permute-start | bytes 294920 | tf_op jit(solution)/shard_map/ppermute | solution.py:13
  15.2 2.2 copy_multiply_fusion
  17.4 0.7 fusion.61
  20.2 0.8 copy.39
  21.0 1.0 copy.42
  22.0 1.5 pad_maximum_fusion
  24.1 0.7 fusion.38
  25.9 1.5 fusion
  27.5 1.5 fusion.41
  29.0 0.7 fusion.34
  29.8 3.9 %collective-permute-start.4 = (f32[4,16,1,512]{3,0,2,1:T(4,128)S(1)}, f32[4,16,1,512]{3,0,2,1:T(4,128)S(1)}, u32[]{:S(2)}, u32[]{:S(2)}) collective-permute-start(f32[4,16,1,512]{3,0,2,1:T(4,128)S(1)} %get-tuple-element.39), channel_id=1, source_target_pairs={{1,0},{2,1},{3,2},{4,3},{5,4},{6,5},{7,6},{8,7},{9,8},{10,9},{11,1... | collective-permute-start | bytes 393224 | tf_op jit(solution)/shard_map/ppermute | solution.py:25
  34.0 2.2 collective-permute-done.4
  36.2 4.6 %collective-permute-done.3 = f32[4,16,1,512]{3,0,2,1:T(4,128)S(1)} collective-permute-done((f32[4,16,1,512]{3,0,2,1:T(4,128)S(1)}, f32[4,16,1,512]{3,0,2,1:T(4,128)S(1)}, u32[]{:S(2)}, u32[]{:S(2)}) %collective-permute-start.3) | collective-permute-done | bytes 131104 | tf_op jit(solution)/shard_map/ppermute | solution.py:22
  41.3 1.1 fusion.37
  42.4 0.7 fusion.30
  44.0 1.7 collective-permute-done.6
  45.8 4.8 %collective-permute-done.5 = f32[4,16,1,512]{3,0,2,1:T(4,128)S(1)} collective-permute-done((f32[4,16,1,512]{3,0,2,1:T(4,128)S(1)}, f32[4,16,1,512]{3,0,2,1:T(4,128)S(1)}, u32[]{:S(2)}, u32[]{:S(2)}) %collective-permute-start.5) | collective-permute-done | bytes 131104 | tf_op jit(solution)/shard_map/ppermute | solution.py:22
  51.1 1.1 fusion.33
  52.2 0.7 fusion.26
  53.8 1.7 collective-permute-done.8
  55.6 4.6 %collective-permute-done.7 = f32[4,16,1,512]{3,0,2,1:T(4,128)S(1)} collective-permute-done((f32[4,16,1,512]{3,0,2,1:T(4,128)S(1)}, f32[4,16,1,512]{3,0,2,1:T(4,128)S(1)}, u32[]{:S(2)}, u32[]{:S(2)}) %collective-permute-start.7) | collective-permute-done | bytes 131104 | tf_op jit(solution)/shard_map/ppermute | solution.py:22
  60.7 1.0 fusion.29
  61.8 5.9 %copy.54 = f32[4,16,8,512]{1,0,3,2:T(4,128)} copy(f32[4,16,8,512]{3,0,2,1:T(4,128)S(1)} %fusion.29) | data formatting | bytes 2097152 | tf_op jit(solution)/shard_map/reshape | solution.py:95
  67.7 5.8 %gather_fusion = f32[512,4,16]{2,1,0:T(4,128)} fusion(f32[4,16,4096]{1,0,2:T(4,128)} %bitcast.43, s32[1024]{0:T(1024)S(1)} %pad_clamp_fusion), kind=kCustom, calls=%fused_computation | custom fusion | bytes 264192 | tf_op jit(solution)/shard_map/jit(_take)/gather | solution.py:100
  73.5 9.0 %fusion.42 = f32[4,512]{0,1:T(8,128)} fusion(f32[512,4,16]{2,1,0:T(4,128)} %gather_fusion, f32[16,512]{0,1:T(8,128)} %copy.39, pred[512]{0:T(512)(128)(4,1)S(1)} %copy-done.17), kind=kLoop, calls=%fused_computation.83 | loop fusion | flops 96256 | bytes 172544 | tf_op jit(solution)/shard_map/reduce_sum | solution.py:104
  82.5 1.1 copy.55
  83.7 0.7 all_to_all.20
  84.4 3.5 %all-to-all-start.1 = ((f32[16,1,128]{2,1,0:T(1,128)}), f32[16,1,128]{2,1,0:T(1,128)S(1)}, u32[]{:S(2)}, u32[]{:S(2)}) async-start(f32[16,1,128]{2,1,0:T(1,128)} %bitcast.12), calls=%async_computation.1 | async-start | bytes 16384 | tf_op jit(solution)/shard_map/all_to_all | solution.py:105
  88.0 6.2 %all-to-all-done.1 = f32[16,1,128]{2,1,0:T(1,128)S(1)} async-done(((f32[16,1,128]{2,1,0:T(1,128)}), f32[16,1,128]{2,1,0:T(1,128)S(1)}, u32[]{:S(2)}, u32[]{:S(2)}) %all-to-all-start.1) | async-done | bytes 8224 | tf_op jit(solution)/shard_map/all_to_all | solution.py:105
  94.2 0.6 mul.199
  94.8 3.5 %all-to-all-start.2 = ((f32[16,1,128]{2,1,0:T(1,128)}), f32[16,1,128]{2,1,0:T(1,128)S(1)}, u32[]{:S(2)}, u32[]{:S(2)}) async-start(f32[16,1,128]{2,1,0:T(1,128)} %mul.199), calls=%async_computation.2 | async-start | bytes 16384 | tf_op jit(solution)/shard_map/all_to_all | solution.py:118
  98.4 0.8 copy.38
  99.3 0.8 slice.486
  100.0 0.8 slice.482
  101.4 3.2 %all-to-all-done.2 = f32[16,1,128]{2,1,0:T(1,128)S(1)} async-done(((f32[16,1,128]{2,1,0:T(1,128)}), f32[16,1,128]{2,1,0:T(1,128)S(1)}, u32[]{:S(2)}, u32[]{:S(2)}) %all-to-all-start.2) | async-done | bytes 8224 | tf_op jit(solution)/shard_map/all_to_all | solution.py:118
  105.0 0.7 reduce.4
  105.9 0.9 copy.49
  106.8 4.0 %multiply_multiply_fusion = f32[512,4,16]{2,1,0:T(4,128)S(1)} fusion(f32[512]{0:T(512)S(1)} %reshape.125, f32[512,4]{1,0:T(8,128)} %copy.49, f32[512,16]{1,0:T(8,128)} %copy.38), kind=kLoop, calls=%fused_computation.84 | loop fusion | flops 65536 | bytes 174080 | tf_op jit(solution)/shard_map/mul | solution.py:123
  110.7 4.3 %broadcast_in_dim.14 = f32[4097,4,16]{2,1,0:T(4,128)} broadcast(f32[]{:T(128)} %constant.9.clone.1), dimensions={} | broadcast | bytes 1048836 | tf_op jit(solution)/shard_map/broadcast_in_dim | solution.py:126
  115.1 52.6 %scatter_fusion = f32[4097,4,16]{2,1,0:T(4,128)} fusion(f32[4097,4,16]{2,1,0:T(4,128)} %broadcast_in_dim.14, s32[512]{0:T(512)S(1)} %bitcast.51, f32[512,4,16]{2,1,0:T(4,128)S(1)} %multiply_multiply_fusion), kind=kCustom, calls=%fused_computation.1 | custom fusion | flops 32768 | bytes 395264 | tf_op jit(solution)/shard_map/scatter-add | solution.py:126
  167.7 7.0 %slice.481 = f32[4096,4,16]{2,1,0:T(4,128)} slice(f32[4097,4,16]{2,1,0:T(4,128)} %scatter_fusion), slice={[0:4096], [0:4], [0:16]} | slice | bytes 2097152 | tf_op jit(solution)/shard_map/slice | solution.py:126
  174.7 6.7 %copy.51 = f32[8,512,4,16]{1,2,0,3:T(4,128)S(1)} copy(f32[8,512,4,16]{3,2,1,0:T(4,128)} %bitcast.42) | data formatting | bytes 2097152 | tf_op jit(solution)/shard_map/reshape | solution.py:127
  181.5 1.7 broadcast_multiply_fusion.7
  183.2 4.4 %collective-permute-start.9 = (f32[4,16,1,512]{3,0,2,1:T(4,128)S(1)}, f32[4,16,1,512]{3,0,2,1:T(4,128)S(1)}, u32[]{:S(2)}, u32[]{:S(2)}) collective-permute-start(f32[4,16,1,512]{3,0,2,1:T(4,128)S(1)} %get-tuple-element.34), channel_id=1, source_target_pairs={{1,0},{2,1},{3,2},{4,3},{5,4},{6,5},{7,6},{8,7},{9,8},{10,9},{11,1... | collective-permute-start | bytes 393224 | tf_op jit(solution)/shard_map/ppermute | solution.py:25
  188.0 2.3 collective-permute-done.10
  190.7 1.7 fusion.24
  192.4 0.9 broadcast_multiply_fusion.6
  193.3 4.5 %collective-permute-start.11 = (f32[4,16,1,512]{3,0,2,1:T(4,128)S(1)}, f32[4,16,1,512]{3,0,2,1:T(4,128)S(1)}, u32[]{:S(2)}, u32[]{:S(2)}) collective-permute-start(f32[4,16,1,512]{3,0,2,1:T(4,128)S(1)} %get-tuple-element.30), channel_id=1, source_target_pairs={{1,0},{2,1},{3,2},{4,3},{5,4},{6,5},{7,6},{8,7},{9,8},{10,9},{11,1... | collective-permute-start | bytes 393224 | tf_op jit(solution)/shard_map/ppermute | solution.py:25
  198.1 2.3 collective-permute-done.12
  200.7 1.7 fusion.19
  202.5 0.9 broadcast_multiply_fusion.5
  203.4 4.6 %collective-permute-start.13 = (f32[4,16,1,512]{3,0,2,1:T(4,128)S(1)}, f32[4,16,1,512]{3,0,2,1:T(4,128)S(1)}, u32[]{:S(2)}, u32[]{:S(2)}) collective-permute-start(f32[4,16,1,512]{3,0,2,1:T(4,128)S(1)} %get-tuple-element.26), channel_id=1, source_target_pairs={{1,0},{2,1},{3,2},{4,3},{5,4},{6,5},{7,6},{8,7},{9,8},{10,9},{11,1... | collective-permute-start | bytes 393224 | tf_op jit(solution)/shard_map/ppermute | solution.py:25
  208.3 2.3 collective-permute-done.14
  210.9 1.7 fusion.14
  212.6 0.9 broadcast_multiply_fusion.4
  213.6 4.6 %collective-permute-start.15 = (f32[4,16,1,512]{3,0,2,1:T(4,128)S(1)}, f32[4,16,1,512]{3,0,2,1:T(4,128)S(1)}, u32[]{:S(2)}, u32[]{:S(2)}) collective-permute-start(f32[4,16,1,512]{3,0,2,1:T(4,128)S(1)} %get-tuple-element.22), channel_id=1, source_target_pairs={{1,0},{2,1},{3,2},{4,3},{5,4},{6,5},{7,6},{8,7},{9,8},{10,9},{11,1... | collective-permute-start | bytes 393224 | tf_op jit(solution)/shard_map/ppermute | solution.py:25
  218.4 2.3 collective-permute-done.16
  221.1 2.6 fusion.9
  223.7 1.3 copy.53
  224.9 1.1 convolution_bitcast_fusion
  226.1 34.0 %psum.7 = f32[4,128]{1,0:T(4,128)S(1)} all-reduce(f32[4,128]{1,0:T(4,128)S(1)} %convolution_bitcast_fusion), channel_id=1, replica_groups=mesh['groups'=2,'cells'=16] {'cells'}, use_global_device_ids=true, to_apply=%region_2.3 | all-reduce | flops 512 | bytes 4096 | tf_op jit(solution)/shard_map/psum | solution.py:135
  (109 shorter events, 12.2 us)
Async XLA Ops:
  0.6 224.3 %copy-start = (f32[8,512,128]{2,1,0:T(8,128)S(1)}, f32[8,512,128]{2,1,0:T(8,128)}, u32[]{:S(2)}) copy-start(f32[8,512,128]{2,1,0:T(8,128)} %param.11) | copy-start | bytes 6291460
  2.2 17.7 %all-to-all-start = ((f32[16,1,512]{2,1,0:T(1,128)}), f32[16,1,512]{2,1,0:T(1,128)S(1)}, u32[]{:S(2)}, u32[]{:S(2)}) async-start(f32[16,1,512]{2,1,0:T(1,128)} %all_to_all.18), calls=%async_computation | async-start | bytes 65536 | tf_op jit(solution)/shard_map/all_to_all | solution.py:88
  10.8 7.9 %copy-start.15 = (s32[16,32]{1,0:T(8,128)S(1)}, s32[16,32]{1,0:T(8,128)}, u32[]{:S(2)}) copy-start(s32[16,32]{1,0:T(8,128)} %param.15) | copy-start | bytes 6148
  10.8 10.2 %collective-permute-start = (f32[3,16,1,512]{3,1,2,0:T(8,128)S(1)}, f32[3,16,1,512]{3,1,2,0:T(8,128)}, u32[]{:S(2)}, u32[]{:S(2)}) collective-permute-start(f32[3,16,1,512]{3,1,2,0:T(8,128)S(1)} %copy.59), channel_id=1, source_target_pairs={{0,15},{1,0},{2,1},{3,2},{4,3},{5,4},{6,5},{7,6},{8,7},{9,8},{10,9... | collective-permute-start | bytes 294920 | tf_op jit(solution)/shard_map/ppermute | solution.py:13
  18.1 7.2 %collective-permute-start.2 = (f32[4,16,1,512]{3,0,2,1:T(4,128)}, f32[4,16,1,512]{3,0,2,1:T(4,128)}, u32[]{:S(2)}, u32[]{:S(2)}) collective-permute-start(f32[4,16,1,512]{3,0,2,1:T(4,128)} %get-tuple-element.41), channel_id=1, source_target_pairs={{1,0},{2,1},{3,2},{4,3},{5,4},{6,5},{7,6},{8,7},{9,8},{10,9},{11,1... | collective-permute-start | bytes 393224 | tf_op jit(solution)/shard_map/ppermute | solution.py:25
  18.5 7.4 %collective-permute-start.1 = (f32[4,16,1,512]{3,0,2,1:T(4,128)}, f32[4,16,1,512]{3,0,2,1:T(4,128)}, u32[]{:S(2)}, u32[]{:S(2)}) collective-permute-start(f32[4,16,1,512]{3,0,2,1:T(4,128)} %get-tuple-element.42), channel_id=1, source_target_pairs={{0,1},{1,2},{2,3},{3,4},{4,5},{5,6},{6,7},{7,8},{8,9},{9,10},{10,1... | collective-permute-start | bytes 393224 | tf_op jit(solution)/shard_map/ppermute | solution.py:22
  23.8 1.3 copy-start.11
  23.8 1.4 copy-start.9
  23.9 29.6 %copy-start.3 = (f32[15,8,512]{2,1,0:T(8,128)}, f32[15,8,512]{2,1,0:T(8,128)S(1)}, u32[]{:S(2)}) copy-start(f32[15,8,512]{2,1,0:T(8,128)S(1)} %slice.454) | copy-start | bytes 737284
  24.1 28.1 %copy-start.1 = (f32[16,8,511]{2,1,0:T(8,128)}, f32[16,8,511]{2,1,0:T(8,128)S(1)}, u32[]{:S(2)}) copy-start(f32[16,8,511]{2,1,0:T(8,128)S(1)} %get-tuple-element.44) | copy-start | bytes 784900
  25.3 2.2 copy-start.5
  25.3 2.2 copy-start.13
  29.8 6.4 %collective-permute-start.4 = (f32[4,16,1,512]{3,0,2,1:T(4,128)S(1)}, f32[4,16,1,512]{3,0,2,1:T(4,128)S(1)}, u32[]{:S(2)}, u32[]{:S(2)}) collective-permute-start(f32[4,16,1,512]{3,0,2,1:T(4,128)S(1)} %get-tuple-element.39), channel_id=1, source_target_pairs={{1,0},{2,1},{3,2},{4,3},{5,4},{6,5},{7,6},{8,7},{9,8},{10,9},{11,1... | collective-permute-start | bytes 393224 | tf_op jit(solution)/shard_map/ppermute | solution.py:25
  33.7 7.1 %collective-permute-start.3 = (f32[4,16,1,512]{3,0,2,1:T(4,128)S(1)}, f32[4,16,1,512]{3,0,2,1:T(4,128)S(1)}, u32[]{:S(2)}, u32[]{:S(2)}) collective-permute-start(f32[4,16,1,512]{3,0,2,1:T(4,128)S(1)} %get-tuple-element.40), channel_id=1, source_target_pairs={{0,1},{1,2},{2,3},{3,4},{4,5},{5,6},{6,7},{7,8},{8,9},{9,10},{10,1... | collective-permute-start | bytes 393224 | tf_op jit(solution)/shard_map/ppermute | solution.py:22
  43.2 2.6 collective-permute-start.6
  43.2 7.3 %collective-permute-start.5 = (f32[4,16,1,512]{3,0,2,1:T(4,128)S(1)}, f32[4,16,1,512]{3,0,2,1:T(4,128)S(1)}, u32[]{:S(2)}, u32[]{:S(2)}) collective-permute-start(f32[4,16,1,512]{3,0,2,1:T(4,128)S(1)} %get-tuple-element.38), channel_id=1, source_target_pairs={{0,1},{1,2},{2,3},{3,4},{4,5},{5,6},{6,7},{7,8},{8,9},{9,10},{10,1... | collective-permute-start | bytes 393224 | tf_op jit(solution)/shard_map/ppermute | solution.py:22
  53.0 2.6 collective-permute-start.8
  53.0 7.1 %collective-permute-start.7 = (f32[4,16,1,512]{3,0,2,1:T(4,128)S(1)}, f32[4,16,1,512]{3,0,2,1:T(4,128)S(1)}, u32[]{:S(2)}, u32[]{:S(2)}) collective-permute-start(f32[4,16,1,512]{3,0,2,1:T(4,128)S(1)} %get-tuple-element.36), channel_id=1, source_target_pairs={{0,1},{1,2},{2,3},{3,4},{4,5},{5,6},{6,7},{7,8},{8,9},{9,10},{10,1... | collective-permute-start | bytes 393224 | tf_op jit(solution)/shard_map/ppermute | solution.py:22
  61.8 11.7 %copy-start.17 = (pred[512]{0:T(512)(128)(4,1)S(1)}, pred[512]{0:T(512)(128)(4,1)}, u32[]{:S(2)}) copy-start(pred[512]{0:T(512)(128)(4,1)} %le.16) | copy-start | bytes 1540
  67.7 20.2 %copy-start.16 = (f32[16,32]{1,0:T(8,128)S(1)}, f32[16,32]{1,0:T(8,128)}, u32[]{:S(2)}) copy-start(f32[16,32]{1,0:T(8,128)} %param.14) | copy-start | bytes 6148
  67.7 30.6 %copy-start.18 = (f32[128]{0:T(128)S(1)}, f32[128]{0:T(128)}, u32[]{:S(2)}) copy-start(f32[128]{0:T(128)} %param.12) | copy-start | bytes 1540
  73.5 25.8 %copy-start.12 = (f32[16,10,512]{2,1,0:T(8,128)S(1)}, f32[16,10,512]{2,1,0:T(8,128)}, u32[]{:S(2)}) copy-start(f32[16,10,512]{2,1,0:T(8,128)} %copy-done.11) | copy-start | bytes 983044
  73.5 26.5 %copy-start.10 = (f32[16,10,512]{2,1,0:T(8,128)S(1)}, f32[16,10,512]{2,1,0:T(8,128)}, u32[]{:S(2)}) copy-start(f32[16,10,512]{2,1,0:T(8,128)} %copy-done.9) | copy-start | bytes 983044
  84.4 9.8 %all-to-all-start.1 = ((f32[16,1,128]{2,1,0:T(1,128)}), f32[16,1,128]{2,1,0:T(1,128)S(1)}, u32[]{:S(2)}, u32[]{:S(2)}) async-start(f32[16,1,128]{2,1,0:T(1,128)} %bitcast.12), calls=%async_computation.1 | async-start | bytes 16384 | tf_op jit(solution)/shard_map/all_to_all | solution.py:105
  94.8 9.8 %all-to-all-start.2 = ((f32[16,1,128]{2,1,0:T(1,128)}), f32[16,1,128]{2,1,0:T(1,128)S(1)}, u32[]{:S(2)}, u32[]{:S(2)}) async-start(f32[16,1,128]{2,1,0:T(1,128)} %mul.199), calls=%async_computation.2 | async-start | bytes 16384 | tf_op jit(solution)/shard_map/all_to_all | solution.py:118
  181.4 6.2 %copy-start.4 = (f32[15,8,512]{2,1,0:T(8,128)S(1)}, f32[15,8,512]{2,1,0:T(8,128)}, u32[]{:S(2)}) copy-start(f32[15,8,512]{2,1,0:T(8,128)} %copy-done.3) | copy-start | bytes 737284
  183.2 7.1 %collective-permute-start.10 = (f32[4,16,1,512]{3,0,2,1:T(4,128)S(1)}, f32[4,16,1,512]{3,0,2,1:T(4,128)S(1)}, u32[]{:S(2)}, u32[]{:S(2)}) collective-permute-start(f32[4,16,1,512]{3,0,2,1:T(4,128)S(1)} %get-tuple-element.33), channel_id=1, source_target_pairs={{0,1},{1,2},{2,3},{3,4},{4,5},{5,6},{6,7},{7,8},{8,9},{9,10},{10,1... | collective-permute-start | bytes 393224 | tf_op jit(solution)/shard_map/ppermute | solution.py:22
  183.2 7.1 %collective-permute-start.9 = (f32[4,16,1,512]{3,0,2,1:T(4,128)S(1)}, f32[4,16,1,512]{3,0,2,1:T(4,128)S(1)}, u32[]{:S(2)}, u32[]{:S(2)}) collective-permute-start(f32[4,16,1,512]{3,0,2,1:T(4,128)S(1)} %get-tuple-element.34), channel_id=1, source_target_pairs={{1,0},{2,1},{3,2},{4,3},{5,4},{6,5},{7,6},{8,7},{9,8},{10,9},{11,1... | collective-permute-start | bytes 393224 | tf_op jit(solution)/shard_map/ppermute | solution.py:25
  188.0 2.7 %copy-start.7 = (f32[16,8,512]{2,1,0:T(8,128)S(1)}, f32[16,8,512]{2,1,0:T(8,128)}, u32[]{:S(2)}) copy-start(f32[16,8,512]{2,1,0:T(8,128)} %slice.486) | copy-start | bytes 786436
  188.0 2.7 %copy-start.8 = (f32[16,8,512]{2,1,0:T(8,128)S(1)}, f32[16,8,512]{2,1,0:T(8,128)}, u32[]{:S(2)}) copy-start(f32[16,8,512]{2,1,0:T(8,128)} %slice.482) | copy-start | bytes 786436
  190.7 1.7 copy-start.2
  193.3 7.1 %collective-permute-start.12 = (f32[4,16,1,512]{3,0,2,1:T(4,128)S(1)}, f32[4,16,1,512]{3,0,2,1:T(4,128)S(1)}, u32[]{:S(2)}, u32[]{:S(2)}) collective-permute-start(f32[4,16,1,512]{3,0,2,1:T(4,128)S(1)} %get-tuple-element.29), channel_id=1, source_target_pairs={{0,1},{1,2},{2,3},{3,4},{4,5},{5,6},{6,7},{7,8},{8,9},{9,10},{10,1... | collective-permute-start | bytes 393224 | tf_op jit(solution)/shard_map/ppermute | solution.py:22
  193.3 7.1 %collective-permute-start.11 = (f32[4,16,1,512]{3,0,2,1:T(4,128)S(1)}, f32[4,16,1,512]{3,0,2,1:T(4,128)S(1)}, u32[]{:S(2)}, u32[]{:S(2)}) collective-permute-start(f32[4,16,1,512]{3,0,2,1:T(4,128)S(1)} %get-tuple-element.30), channel_id=1, source_target_pairs={{1,0},{2,1},{3,2},{4,3},{5,4},{6,5},{7,6},{8,7},{9,8},{10,9},{11,1... | collective-permute-start | bytes 393224 | tf_op jit(solution)/shard_map/ppermute | solution.py:25
  203.4 7.2 %collective-permute-start.14 = (f32[4,16,1,512]{3,0,2,1:T(4,128)S(1)}, f32[4,16,1,512]{3,0,2,1:T(4,128)S(1)}, u32[]{:S(2)}, u32[]{:S(2)}) collective-permute-start(f32[4,16,1,512]{3,0,2,1:T(4,128)S(1)} %get-tuple-element.25), channel_id=1, source_target_pairs={{0,1},{1,2},{2,3},{3,4},{4,5},{5,6},{6,7},{7,8},{8,9},{9,10},{10,1... | collective-permute-start | bytes 393224 | tf_op jit(solution)/shard_map/ppermute | solution.py:22
  203.4 7.1 %collective-permute-start.13 = (f32[4,16,1,512]{3,0,2,1:T(4,128)S(1)}, f32[4,16,1,512]{3,0,2,1:T(4,128)S(1)}, u32[]{:S(2)}, u32[]{:S(2)}) collective-permute-start(f32[4,16,1,512]{3,0,2,1:T(4,128)S(1)} %get-tuple-element.26), channel_id=1, source_target_pairs={{1,0},{2,1},{3,2},{4,3},{5,4},{6,5},{7,6},{8,7},{9,8},{10,9},{11,1... | collective-permute-start | bytes 393224 | tf_op jit(solution)/shard_map/ppermute | solution.py:25
  213.5 7.2 %collective-permute-start.16 = (f32[4,16,1,512]{3,0,2,1:T(4,128)S(1)}, f32[4,16,1,512]{3,0,2,1:T(4,128)S(1)}, u32[]{:S(2)}, u32[]{:S(2)}) collective-permute-start(f32[4,16,1,512]{3,0,2,1:T(4,128)S(1)} %get-tuple-element.21), channel_id=1, source_target_pairs={{0,1},{1,2},{2,3},{3,4},{4,5},{5,6},{6,7},{7,8},{8,9},{9,10},{10,1... | collective-permute-start | bytes 393224 | tf_op jit(solution)/shard_map/ppermute | solution.py:22
  213.6 7.1 %collective-permute-start.15 = (f32[4,16,1,512]{3,0,2,1:T(4,128)S(1)}, f32[4,16,1,512]{3,0,2,1:T(4,128)S(1)}, u32[]{:S(2)}, u32[]{:S(2)}) collective-permute-start(f32[4,16,1,512]{3,0,2,1:T(4,128)S(1)} %get-tuple-element.22), channel_id=1, source_target_pairs={{1,0},{2,1},{3,2},{4,3},{5,4},{6,5},{7,6},{8,7},{9,8},{10,9},{11,1... | collective-permute-start | bytes 393224 | tf_op jit(solution)/shard_map/ppermute | solution.py:25
  218.4 2.6 %copy-start.6 = (f32[4,16,8,512]{3,2,1,0:T(8,128)S(1)}, f32[4,16,8,512]{3,2,1,0:T(8,128)}, u32[]{:S(2)}) copy-start(f32[4,16,8,512]{3,2,1,0:T(8,128)} %param.8) | copy-start | bytes 3145732
  218.4 2.6 %copy-start.14 = (f32[16,8,512]{2,1,0:T(8,128)S(1)}, f32[16,8,512]{2,1,0:T(8,128)}, u32[]{:S(2)}) copy-start(f32[16,8,512]{2,1,0:T(8,128)} %param.10) | copy-start | bytes 786436
where the time goes:
time: 262 us; the launch traced here: 261 us
  other arithmetic  98.7 us (38%)
  local copies, waits for them, and re-layouts  44.2 us (17%)
  starting transfers between devices  42.5 us (16%)
  waiting for transfers between devices  38.8 us (15%)
  blocking collectives  34 us (13%)
    scatter-add x1, other arithmetic, local(): jax.ops.segment_sum(stacked, segment_ids, num_segments=cells_tile + 1)  52.6 us
    psum x1, blocking collectives, local(): projection = lax.psum(partial_sums, 'cells')  34 us
    ppermute x8, waiting for transfers between devices, padded(): lax.ppermute(lax.slice_in_dim(block, block.shape[dim] - width, None, axis...  23.8 us
    ppermute x8, starting transfers between devices, padded(): lax.ppermute(lax.slice_in_dim(block, 0, width, axis=dim), axis, backward)  22.4 us
    reduce_sum x1, other arithmetic, local(): modeled = jnp.sum(kernel_slots[None] * sampled, axis=1) * present_f  9.04 us
    all_to_all x1, starting transfers between devices, local(): lax.all_to_all(kernel_rows, 'cells', split_axis=0, concat_axis=0, tiled=T...  7.39 us
    slice x1, local copies, waits for them, and re-layouts, local(): jax.ops.segment_sum(stacked, segment_ids, num_segments=cells_tile + 1)  7.03 us
    reshape x1, local copies, waits for them, and re-layouts, local(): summed.reshape(lon_width, lat_rows, probe_count, LEV).transpose(2, 3, 0, 1)  6.73 us
  transfers between devices with their start and end apart: 20, of which 13 were waited for; matrix products, arithmetic and copies ran while one was open for 6% of the time, Pallas kernels for 0%

commit v1 on v0

v1 whole, which is shorter than its diff:
```python
import functools

import jax
import jax.numpy as jnp
from jax import lax
from jax.experimental import pallas as pl
from jax.experimental.pallas import tpu as pltpu
from jax.sharding import PartitionSpec as P

MESH = pl.DeviceIdType.MESH
HIGHEST = lax.Precision.HIGHEST
LEV = 16
STEPS = 4
CAP = 32
LANES = 128
HALO = STEPS


def split_bf16(value):
    high = value.astype(jnp.bfloat16)
    low = (value - high.astype(jnp.float32)).astype(jnp.bfloat16)
    return high, low


def kernel(
    probes, wind, prior, basis, eigen_values, kernel_rows, obs_weight, tile_column,
    hess_out, misfit_out, coeffs_out,
    probes_v, wind_v, prior_v, basis_v, basis_split, hess_v,
    fwd, adj, east, north_mix, row_send, row_recv, rows_2d, slots, weighted, one_hot, sampled,
    mis_2d, mis_send, mis_recv, proj, proj_recv,
    load_sem, col_send, col_recv, row_ssem, row_rsem, slot_ssem, slot_rsem, wt_ssem, wt_rsem,
    mis_ssem, mis_rsem, proj_ssem, proj_rsem,
):
    group = lax.axis_index("groups")
    me = lax.axis_index("cells")
    n = lax.axis_size("cells")
    east_nbr = lax.rem(me + 1, n)
    west_nbr = lax.rem(me + n - 1, n)
    lat = probes.shape[1]
    lon = fwd.shape[1] - 2 * HALO
    probe_count = fwd.shape[2] // LEV
    rows = probe_count * LEV
    total = n * CAP
    per_probe = LEV * lon

    barrier = pltpu.get_barrier_semaphore()

    def greet(i, carry):
        pl.semaphore_signal(
            barrier, inc=1, device_id=(group, lax.rem(me + i, n)), device_id_type=MESH
        )
        return carry

    lax.fori_loop(1, n, greet, 0)

    def tile_loads(source, target, at):
        return [
            pltpu.make_async_copy(
                source.at[:, pl.ds(t * LANES, LANES)], target.at[t], load_sem.at[at, t]
            )
            for t in range(lat // LANES)
        ]

    loads = [
        tile_loads(prior, prior_v, 0),
        tile_loads(probes, probes_v, 1),
        tile_loads(wind, wind_v, 2),
        [pltpu.make_async_copy(basis, basis_v, load_sem.at[3, 0])],
    ]
    for load in loads:
        for piece in load:
            piece.start()

    def wait_loads(at):
        for piece in loads[at]:
            piece.wait()

    def column(ref, base, i):
        return jnp.concatenate(
            [ref[t, pl.ds(base + i, LEV, stride=lon), :] for t in range(lat // LANES)], axis=1
        )

    def stage_row(i, carry):
        row_send[i, :, 0 : LEV * CAP] = kernel_rows[pl.ds(i, 1), :]
        row_send[i, :, LEV * CAP : LEV * CAP + CAP] = obs_weight[pl.ds(i, 1), :]
        row_send[i, :, LEV * CAP + CAP :] = jnp.zeros((1, LANES - CAP), jnp.float32)
        return carry

    lax.fori_loop(0, n, stage_row, 0)

    wait_loads(0)
    wait_loads(1)

    def start_col(i):
        scale = column(prior_v, 0, i)
        for k in range(probe_count):
            fwd[0, HALO + i, k * LEV : (k + 1) * LEV, :] = (
                scale * column(probes_v, k * per_probe, i)
            )

    def wind_col(i):
        level = lax.broadcasted_iota(jnp.int32, (LEV, lat), 0)
        row = lax.broadcasted_iota(jnp.int32, (LEV, lat), 1)
        east[HALO + i] = 0.3 * column(wind_v, 0, i)
        north_mix[HALO + i, 0] = jnp.where(
            row == 0, 0.0, 0.15 * column(wind_v, per_probe, i)
        )
        north_mix[HALO + i, 1] = jnp.where(
            level == 0, 0.0, 0.025 * (1.0 + column(wind_v, 2 * per_probe, i))
        )

    edges = []
    for d in range(HALO):
        edges += [lon - 1 - d, d]
    for i in edges:
        start_col(i)
    wait_loads(2)
    for i in edges:
        wind_col(i)

    pl.semaphore_wait(barrier, n - 1)

    def row_copy(target, source_id):
        return pltpu.make_async_remote_copy(
            src_ref=row_send.at[target], dst_ref=row_recv.at[source_id],
            send_sem=row_ssem.at[target], recv_sem=row_rsem.at[source_id],
            device_id=(group, target), device_id_type=MESH,
        )

    def send_row(i, carry):
        row_copy(lax.rem(me + i, n), me).start()
        return carry

    lax.fori_loop(1, n, send_row, 0)

    arrays = (fwd.at[0], east, north_mix)

    def column_copy(kind, side, d):
        if side == 0:
            source, target, device = HALO + lon - 1 - d, HALO - 1 - d, east_nbr
        else:
            source, target, device = HALO + d, HALO + lon + d, west_nbr
        return pltpu.make_async_remote_copy(
            src_ref=arrays[kind].at[source], dst_ref=arrays[kind].at[target],
            send_sem=col_send.at[kind, side, d], recv_sem=col_recv.at[kind, side, d],
            device_id=(group, device), device_id_type=MESH,
        )

    sends = []
    for d in range(HALO):
        for kind in range(3):
            if kind == 2 and d == HALO - 1:
                continue
            for side in range(2):
                if kind == 1 and d == HALO - 1 and side == 0:
                    continue
                sends.append(column_copy(kind, side, d))
                sends[-1].start()

    def forward_col(s, e):
        east_here = east[e]
        east_next = east[e + 1]
        north = north_mix[e, 0]
        mixing = north_mix[e, 1]
        for k in range(probe_count):
            part = pl.ds(k * LEV, LEV)
            center = fwd[s, e, part, :]
            flux = east_here * jnp.where(east_here > 0.0, fwd[s, e - 1, part, :], center)
            flux_next = east_next * jnp.where(east_next > 0.0, center, fwd[s, e + 1, part, :])
            south = north * jnp.where(north > 0.0, pltpu.roll(center, 1, 1), center)
            up = mixing * (pltpu.roll(center, 1, 0) - center)
            fwd[s + 1, e, part, :] = (
                center - (flux_next - flux) - (pltpu.roll(south, lat - 1, 1) - south)
                + (up - pltpu.roll(up, LEV - 1, 0))
            )

    def backward_col(s, e):
        east_neg = jnp.minimum(east[e], 0.0)
        east_pos = jnp.maximum(east[e + 1], 0.0)
        north = north_mix[e, 0]
        mixing = north_mix[e, 1]
        north_pos = jnp.maximum(north, 0.0)
        north_neg = jnp.minimum(north, 0.0)
        for k in range(probe_count):
            part = pl.ds(k * LEV, LEV)
            center = adj[s, e, part, :]
            diff = center - pltpu.roll(center, 1, 1)
            up = mixing * (pltpu.roll(center, 1, 0) - center)
            adj[s + 1, e, part, :] = (
                center
                + east_pos * (adj[s, e + 1, part, :] - center)
                + east_neg * (center - adj[s, e - 1, part, :])
                + pltpu.roll(north_pos * diff, lat - 1, 1) + north_neg * diff
                + (up - pltpu.roll(up, LEV - 1, 0))
            )

    def interior(col):
        for s in range(STEPS - 1):
            def body(i, carry, s=s):
                col(s, HALO + i)
                return carry

            lax.fori_loop(s + 1, lon - 1 - s, body, 0)

    def diagonal(col, d):
        def body(s, carry):
            col(s, HALO - d + s)
            col(s, HALO + lon - 1 + d - s)
            return carry

        lax.fori_loop(0, STEPS, body, 0)

    for i in range(HALO, lon - HALO):
        start_col(i)
        wind_col(i)
    interior(forward_col)

    row_recv[me] = row_send[me]

    def row_arrival(i, carry):
        source = lax.rem(me + i, n)
        row_copy(source, source).wait_recv()
        return carry

    lax.fori_loop(1, n, row_arrival, 0)

    def flatten_row(i, carry):
        rows_2d[pl.ds(i, 1), :] = row_recv[i]
        return carry

    lax.fori_loop(0, n, flatten_row, 0)

    slot_id = lax.broadcasted_iota(jnp.int32, (n, total), 1)
    holder = lax.broadcasted_iota(jnp.int32, (n, total), 0)
    held = (slot_id >> 5) == holder

    def spread(block, offset):
        lane = lax.broadcasted_iota(jnp.int32, (block.shape[1], total), 0)
        slot = lax.broadcasted_iota(jnp.int32, (block.shape[1], total), 1)
        pick = jnp.where(lane == (slot & (CAP - 1)) + offset, 1.0, 0.0)
        wide = jnp.dot(block, pick, precision=HIGHEST, preferred_element_type=jnp.float32)
        return jnp.sum(jnp.where(held, wide, 0.0), axis=0, keepdims=True)

    for level in range(LEV):
        tile = level * CAP // LANES
        slots[0, level : level + 1, :] = spread(
            rows_2d[:, tile * LANES : (tile + 1) * LANES], level * CAP % LANES
        )
    weight_row = spread(rows_2d[:, LEV * CAP :], 0)
    slots[0, LEV : LEV + 1, :] = spread(tile_column[...].astype(jnp.float32), 0)
    slots[0, LEV + 1 :, :] = jnp.zeros((slots.shape[1] - LEV - 1, total), jnp.float32)

    def slot_copy(side):
        return pltpu.make_async_remote_copy(
            src_ref=slots.at[0], dst_ref=slots.at[1 + side],
            send_sem=slot_ssem.at[side], recv_sem=slot_rsem.at[side],
            device_id=(group, (east_nbr, west_nbr)[side]), device_id_type=MESH,
        )

    for side in range(2):
        sends.append(slot_copy(side))
        sends[-1].start()

    def columns_of(which):
        column = slots[which, LEV : LEV + 1, :].astype(jnp.int32)
        return column, column >> (lat.bit_length() - 1)

    def make_one_hot(which):
        column, _ = columns_of(which)
        row = jnp.where(column < 0, -1, column & (lat - 1))
        place = lax.broadcasted_iota(jnp.int32, (lat, total), 0)
        one_hot[which] = jnp.where(place == row, 1.0, 0.0).astype(jnp.bfloat16)

    make_one_hot(0)
    sampled[...] = jnp.zeros_like(sampled)
    wait_loads(3)

    def split_basis(i, carry):
        high, low = split_bf16(basis_v[i])
        basis_split[i, :, 0:LANES] = high
        basis_split[i, :, LANES:] = low
        return carry

    lax.fori_loop(0, lon, split_basis, 0)

    def forward_diagonal(d, carry):
        for side in range(2):
            pltpu.make_async_remote_copy(
                src_ref=fwd.at[0, 0], dst_ref=fwd.at[0, 0],
                send_sem=col_send.at[0, side, d - 1], recv_sem=col_recv.at[0, side, d - 1],
                device_id=(group, east_nbr), device_id_type=MESH,
            ).wait_recv()

        def wait_wind(kind, side, at):
            pltpu.make_async_remote_copy(
                src_ref=arrays[kind].at[0], dst_ref=arrays[kind].at[0],
                send_sem=col_send.at[kind, side, at], recv_sem=col_recv.at[kind, side, at],
                device_id=(group, east_nbr), device_id_type=MESH,
            ).wait_recv()

        wait_wind(1, 1, d - 1)

        @pl.when(d > 1)
        def _():
            wait_wind(1, 0, d - 2)
            wait_wind(2, 0, d - 2)
            wait_wind(2, 1, d - 2)

        diagonal(forward_col, d - 1)
        pair = (HALO - d, lon - 1 - HALO + d)
        parts = []
        for i in pair:
            parts += split_bf16(fwd[STEPS, HALO + i])
        found = jnp.dot(
            jnp.concatenate(parts, axis=0), one_hot[0], preferred_element_type=jnp.float32
        )
        _, lon_row = columns_of(0)
        picked = sampled[...]
        for at, i in enumerate(pair):
            base = 2 * rows * at
            both = found[base : base + rows] + found[base + rows : base + 2 * rows]
            picked = picked + jnp.where(lon_row == i, both, 0.0)
        sampled[...] = picked
        return carry

    lax.fori_loop(1, HALO + 1, forward_diagonal, 0)

    kernel_slots = slots[0, 0:LEV, :]
    for k in range(probe_count):
        modeled = jnp.sum(
            kernel_slots * sampled[k * LEV : (k + 1) * LEV, :], axis=0, keepdims=True
        )
        weighted[0, k : k + 1, :] = modeled * weight_row

    def weighted_copy(side):
        return pltpu.make_async_remote_copy(
            src_ref=weighted.at[0], dst_ref=weighted.at[1 + side],
            send_sem=wt_ssem.at[side], recv_sem=wt_rsem.at[side],
            device_id=(group, (east_nbr, west_nbr)[side]), device_id_type=MESH,
        )

    for side in range(2):
        sends.append(weighted_copy(side))
        sends[-1].start()

    def inject(which, first_lon, first_ext, count):
        def body(p, carry):
            _, lon_row = columns_of(which)
            levels = slots[which, 0:LEV, :]
            prod = jnp.concatenate(
                [levels * weighted[which, k : k + 1, :] for k in range(probe_count)], axis=0
            )
            parts = []
            for q in range(2):
                parts += split_bf16(jnp.where(lon_row == first_lon + 2 * p + q, prod, 0.0))
            summed = lax.dot_general(
                jnp.concatenate(parts, axis=0), one_hot[which], (((1,), (1,)), ((), ())),
                preferred_element_type=jnp.float32,
            )
            for q in range(2):
                base = 2 * rows * q
                adj[0, first_ext + 2 * p + q] = (
                    summed[base : base + rows] + summed[base + rows : base + 2 * rows]
                )
            return carry

        lax.fori_loop(0, count // 2, body, 0)

    inject(0, 0, HALO, lon)

    gathered = jnp.zeros((n, LANES), jnp.float32)
    for k in range(probe_count):
        slot = lax.broadcasted_iota(jnp.int32, (total, LANES), 0)
        lane = lax.broadcasted_iota(jnp.int32, (total, LANES), 1)
        pick = jnp.where(lane == (slot & (CAP - 1)) + k * CAP, 1.0, 0.0)
        gathered = gathered + jnp.dot(
            jnp.where(held, weighted[0, k : k + 1, :], 0.0), pick,
            precision=HIGHEST, preferred_element_type=jnp.float32,
        )
    mis_2d[...] = gathered

    def mis_copy(target, source_id):
        return pltpu.make_async_remote_copy(
            src_ref=mis_send.at[target], dst_ref=mis_recv.at[source_id],
            send_sem=mis_ssem.at[target], recv_sem=mis_rsem.at[source_id],
            device_id=(group, target), device_id_type=MESH,
        )

    def stage_mis(i, carry):
        mis_send[i] = mis_2d[pl.ds(i, 1), :]
        return carry

    lax.fori_loop(0, n, stage_mis, 0)

    def send_mis(i, carry):
        mis_copy(lax.rem(me + i, n), me).start()
        return carry

    lax.fori_loop(1, n, send_mis, 0)

    for side in range(2):
        slot_copy(side).wait_recv()
        make_one_hot(1 + side)
    interior(backward_col)

    for side in range(2):
        weighted_copy(side).wait_recv()
    inject(1, lon - HALO, 0, HALO)
    inject(2, 0, HALO + lon, HALO)

    proj[...] = jnp.zeros_like(proj)

    def backward_diagonal(d, carry):
        diagonal(backward_col, d - 1)
        for i in (HALO - d, lon - 1 - HALO + d):
            scale = column(prior_v, 0, i)
            lowest = []
            for k in range(probe_count):
                value = (
                    column(probes_v, k * per_probe, i)
                    + scale * adj[STEPS, HALO + i, k * LEV : (k + 1) * LEV, :]
                )
                for t in range(lat // LANES):
                    hess_v[t, pl.ds(k * per_probe + i, LEV, stride=lon), :] = (
                        value[:, t * LANES : (t + 1) * LANES]
                    )
                lowest.append(value[0:1])
            surface = jnp.concatenate(lowest, axis=0)
            high = surface.astype(jnp.bfloat16).astype(jnp.float32)
            stacked = jnp.concatenate(
                [high, surface - high, jnp.zeros((16 - 2 * probe_count, lat), jnp.float32)], axis=0
            ).astype(jnp.bfloat16)
            out = jnp.dot(stacked, basis_split[i], preferred_element_type=jnp.float32)
            proj[0:probe_count, :] = proj[0:probe_count, :] + (
                out[0:probe_count, 0:LANES]
                + (out[0:probe_count, LANES:] + out[probe_count : 2 * probe_count, 0:LANES])
            )
        return carry

    lax.fori_loop(1, HALO + 1, backward_diagonal, 0)

    stores = [
        pltpu.make_async_copy(
            hess_v.at[t], hess_out.at[:, pl.ds(t * LANES, LANES)], load_sem.at[4, t]
        )
        for t in range(lat // LANES)
    ]

    def proj_copy(target, source_id):
        return pltpu.make_async_remote_copy(
            src_ref=proj, dst_ref=proj_recv.at[source_id],
            send_sem=proj_ssem.at[target], recv_sem=proj_rsem.at[source_id],
            device_id=(group, target), device_id_type=MESH,
        )

    def send_proj(i, carry):
        proj_copy(lax.rem(me + i, n), me).start()
        return carry

    lax.fori_loop(1, n, send_proj, 0)
    for store in stores:
        store.start()
    proj_recv[me] = proj[...]

    mis_recv[me] = mis_send[me]

    def mis_arrival(i, carry):
        source = lax.rem(me + i, n)
        mis_copy(source, source).wait_recv()
        return carry

    lax.fori_loop(1, n, mis_arrival, 0)

    def store_mis(i, carry):
        misfit_out[pl.ds(i, 1), :] = mis_recv[i]
        return carry

    lax.fori_loop(0, n, store_mis, 0)

    for store in stores:
        store.wait()
    for copy in sends:
        copy.wait_send()

    def finish(i, carry):
        target = lax.rem(me + i, n)
        row_copy(target, me).wait_send()
        mis_copy(target, me).wait_send()
        return carry

    lax.fori_loop(1, n, finish, 0)

    def proj_arrival(i, carry):
        source = lax.rem(me + i, n)
        proj_copy(source, source).wait_recv()
        proj_copy(source, me).wait_send()
        return carry

    lax.fori_loop(1, n, proj_arrival, 0)
    summed = lax.fori_loop(
        1, n, lambda i, acc: acc + proj_recv[i], proj_recv[0]
    )
    values = eigen_values[...]
    coeffs_out[...] = values / (1.0 + values) * summed[0:probe_count]


def local(
    probes, wind_field, prior_scale, eigen_basis, eigen_values, kernel_rows, obs_weight, tile_column
):
    probe_count, _, lon, lat = probes.shape
    rank = eigen_values.shape[0]
    n = kernel_rows.shape[0]
    rows = probe_count * LEV
    ext = lon + 2 * HALO
    total = n * CAP
    tiles = lat // LANES
    f32 = jnp.float32
    vmem = pl.BlockSpec(memory_space=pltpu.VMEM)
    anywhere = pl.BlockSpec(memory_space=pl.ANY)
    dma = pltpu.SemaphoreType.DMA
    hess, misfit, coeffs = pl.pallas_call(
        kernel,
        out_shape=(
            jax.ShapeDtypeStruct((rows * lon, lat), f32),
            jax.ShapeDtypeStruct((n, probe_count * CAP), f32),
            jax.ShapeDtypeStruct((probe_count, rank), f32),
        ),
        in_specs=[anywhere] * 4 + [vmem] * 4,
        out_specs=(anywhere, vmem, vmem),
        scratch_shapes=[
            pltpu.VMEM((tiles, rows * lon, LANES), f32),
            pltpu.VMEM((tiles, 3 * LEV * lon, LANES), f32),
            pltpu.VMEM((tiles, LEV * lon, LANES), f32),
            pltpu.VMEM((lon, lat, rank), f32),
            pltpu.VMEM((lon, lat, 2 * rank), jnp.bfloat16),
            pltpu.VMEM((tiles, rows * lon, LANES), f32),
            pltpu.VMEM((STEPS + 1, ext, rows, lat), f32),
            pltpu.VMEM((STEPS + 1, ext, rows, lat), f32),
            pltpu.VMEM((ext, LEV, lat), f32),
            pltpu.VMEM((ext, 2, LEV, lat), f32),
            pltpu.VMEM((n, 1, LEV * CAP + LANES), f32),
            pltpu.VMEM((n, 1, LEV * CAP + LANES), f32),
            pltpu.VMEM((n, LEV * CAP + LANES), f32),
            pltpu.VMEM((3, LEV + 8, total), f32),
            pltpu.VMEM((3, 8, total), f32),
            pltpu.VMEM((3, lat, total), jnp.bfloat16),
            pltpu.VMEM((rows, total), f32),
            pltpu.VMEM((n, LANES), f32),
            pltpu.VMEM((n, 1, LANES), f32),
            pltpu.VMEM((n, 1, LANES), f32),
            pltpu.VMEM((8, rank), f32),
            pltpu.VMEM((n, 8, rank), f32),
            dma((5, tiles)),
            dma((3, 2, HALO)),
            dma((3, 2, HALO)),
            dma((n,)),
            dma((n,)),
            dma((2,)),
            dma((2,)),
            dma((2,)),
            dma((2,)),
            dma((n,)),
            dma((n,)),
            dma((n,)),
            dma((n,)),
        ],
        compiler_params=pltpu.CompilerParams(
            collective_id=1, has_side_effects=True, vmem_limit_bytes=56 * 1024 * 1024
        ),
    )(
        probes.reshape(rows * lon, lat),
        wind_field.reshape(3 * LEV * lon, lat),
        prior_scale.reshape(LEV * lon, lat),
        eigen_basis,
        eigen_values.reshape(1, rank),
        kernel_rows,
        obs_weight,
        tile_column,
    )
    return hess.reshape(probes.shape), misfit, coeffs


def solution(mesh):
    in_specs = (
        P("groups", None, "cells", None),
        P(None, None, "cells", None),
        P(None, "cells", None),
        P("cells", None, None),
        P(),
        P(("groups", "cells"), None),
        P(("groups", "cells"), None),
        P(("groups", "cells"), None),
    )
    out_specs = (P("groups", None, "cells", None), P(("groups", "cells"), None), P("groups", None))
    return jax.shard_map(local, mesh=mesh, in_specs=in_specs, out_specs=out_specs, check_vma=False)
```

time: 262 us -> 53 us (0.20)
  other arithmetic: 98.7 us -> 0 us
  Pallas kernels: 0 us -> 48.6 us
  starting transfers between devices: 42.5 us -> 0 us
  local copies, waits for them, and re-layouts: 44.2 us -> 3.45 us
  waiting for transfers between devices: 38.8 us -> 0 us
  blocking collectives: 34 us -> 0 us
    scatter-add x1 -> x0, other arithmetic: 52.6 us -> none  [local(): jax.ops.segment_sum(stacked, segment_ids, num_segments=cells_tile + 1)]
    pallas_call x0 -> x1, Pallas kernels: none -> 48.6 us  [local(): pl.pallas_call(kernel, out_shape=(jax.ShapeDtypeStruct((rows * lon, lat),...]
    psum x1 -> x0, blocking collectives: 34 us -> none  [local(): projection = lax.psum(partial_sums, 'cells')]
    ppermute x17 -> x0, waiting for transfers between devices: 29.4 us -> none  [the longest x8 23.8 us: padded(): lax.ppermute(lax.slice_in_dim(block, block.shape[dim] - width, None, axis...]
    ppermute x17 -> x0, starting transfers between devices: 28.2 us -> none  [the longest x8 22.4 us: padded(): lax.ppermute(lax.slice_in_dim(block, 0, width, axis=dim), axis, backward)]
    add x16 -> x0, other arithmetic: 18.6 us -> none  [the longest x3 5.13 us: backward_step(): return result + vertical_mixing(center, mixing[:, 1:-1])]
    mul x18 -> x0, other arithmetic: 14.8 us -> none  [the longest x4 4.28 us: backward_step(): upper_part = north_pos[..., 1:] * lat_diff]
    all_to_all x3 -> x0, starting transfers between devices: 14.3 us -> none  [the longest x1 7.39 us: local(): lax.all_to_all(kernel_rows, 'cells', split_axis=0, concat_axis=0, tiled=T...]
  transfers between devices with their start and end apart: 20 -> 0, of which waited for: 13 -> 0; matrix products, arithmetic and copies ran while one was open for 6% -> 0% of each run, Pallas kernels for 0% -> 0%
where the time goes in v1:
time: 53 us; the launch traced here: 52.8 us
  Pallas kernels  48.6 us (92%)
  local copies, waits for them, and re-layouts  3.45 us (7%)
  between operations  0.66 us (1%)
    pallas_call x1, Pallas kernels, local(): pl.pallas_call(kernel, out_shape=(jax.ShapeDtypeStruct((rows * lon, lat),...  48.6 us
    unnamed x7, local copies, waits for them, and re-layouts  3.45 us

profile of v1, /device:TPU:0, one launch (start us, length us, event | category | flops | bytes accessed | tf_op | source)
XLA Modules:
  0.0 52.8 jit_solution(7400668848498024857)
XLA Ops:
  0.6 48.6 %shard_map.103 = (f32[512,512]{1,0:T(8,128)}, f32[16,128]{1,0:T(8,128)}, f32[4,128]{1,0:T(4,128)}) custom-call(f32[512,512]{1,0:T(8,128)} %bitcast.5, f32[384,512]{1,0:T(8,128)} %bitcast.7, f32[128,512]{1,0:T(8,128)} %bitcast.8, f32[8,512,128]{2,1,0:T(8,128)} %basis.1, f32[1,128]{1,0:T(1,128)} %bitcast.9, f32[16,512]{1,0:T(8,128)} %kernel_rows.1, ...), custom_call_target="tpu_custom_call" | custom-call | tf_op jit(solution)/shard_map/pallas_call | solution.py:521
  49.3 0.0 copy-start
  49.3 0.0 copy-start.1
  49.3 2.3 %copy.14 = f32[4,16,8,512]{3,2,1,0:T(8,128)} copy(f32[4,16,8,512]{3,2,1,0:T(8,128)} %bitcast.6) | data formatting | bytes 2097152
  51.6 0.0 copy-done
  51.6 0.6 %copy.15 = f32[16,128]{1,0:T(8,128)} copy(f32[16,128]{1,0:T(8,128)S(1)} %copy-done) | data formatting | bytes 16384
  52.2 0.0 copy-done.1
  52.2 0.6 %copy.16 = f32[4,128]{1,0:T(4,128)} copy(f32[4,128]{1,0:T(4,128)S(1)} %copy-done.1) | data formatting | bytes 4096
Async XLA Ops:
  49.3 2.3 %copy-start = (f32[16,128]{1,0:T(8,128)S(1)}, f32[16,128]{1,0:T(8,128)}, u32[]{:S(2)}) copy-start(f32[16,128]{1,0:T(8,128)} %get-tuple-element.13) | copy-start | bytes 24580
  49.3 2.9 %copy-start.1 = (f32[4,128]{1,0:T(4,128)S(1)}, f32[4,128]{1,0:T(4,128)}, u32[]{:S(2)}) copy-start(f32[4,128]{1,0:T(4,128)} %get-tuple-element.14) | copy-start | bytes 6148

commit v2 on v1

--- a/solution.py
+++ b/solution.py
@@ -25,7 +25,7 @@
 def kernel(
     probes, wind, prior, basis, eigen_values, kernel_rows, obs_weight, tile_column,
     hess_out, misfit_out, coeffs_out,
-    probes_v, wind_v, prior_v, basis_v, basis_split, hess_v,
+    probes_v, wind_v, prior_v, basis_v, basis_split, hess_v, to_inner, to_outer,
     fwd, adj, east, north_mix, row_send, row_recv, rows_2d, slots, weighted, one_hot, sampled,
     mis_2d, mis_send, mis_recv, proj, proj_recv,
     load_sem, col_send, col_recv, row_ssem, row_rsem, slot_ssem, slot_rsem, wt_ssem, wt_rsem,
@@ -37,9 +37,10 @@
     east_nbr = lax.rem(me + 1, n)
     west_nbr = lax.rem(me + n - 1, n)
     lat = probes.shape[1]
-    lon = fwd.shape[1] - 2 * HALO
-    probe_count = fwd.shape[2] // LEV
+    lon = fwd[0].shape[0] - 2 * HALO
+    probe_count = fwd[0].shape[2] // LEV
     rows = probe_count * LEV
+    tiles = lat // LANES
     total = n * CAP
     per_probe = LEV * lon
 
@@ -58,7 +59,7 @@
             pltpu.make_async_copy(
                 source.at[:, pl.ds(t * LANES, LANES)], target.at[t], load_sem.at[at, t]
             )
-            for t in range(lat // LANES)
+            for t in range(tiles)
         ]
 
     loads = [
@@ -77,7 +78,7 @@
 
     def column(ref, base, i):
         return jnp.concatenate(
-            [ref[t, pl.ds(base + i, LEV, stride=lon), :] for t in range(lat // LANES)], axis=1
+            [ref[t, pl.ds(base + i, LEV, stride=lon), :] for t in range(tiles)], axis=1
         )
 
     def stage_row(i, carry):
@@ -91,32 +92,54 @@
     wait_loads(0)
     wait_loads(1)
 
-    def start_col(i):
-        scale = column(prior_v, 0, i)
-        for k in range(probe_count):
-            fwd[0, HALO + i, k * LEV : (k + 1) * LEV, :] = (
-                scale * column(probes_v, k * per_probe, i)
-            )
-
-    def wind_col(i):
-        level = lax.broadcasted_iota(jnp.int32, (LEV, lat), 0)
-        row = lax.broadcasted_iota(jnp.int32, (LEV, lat), 1)
-        east[HALO + i] = 0.3 * column(wind_v, 0, i)
-        north_mix[HALO + i, 0] = jnp.where(
-            row == 0, 0.0, 0.15 * column(wind_v, per_probe, i)
-        )
-        north_mix[HALO + i, 1] = jnp.where(
-            level == 0, 0.0, 0.025 * (1.0 + column(wind_v, 2 * per_probe, i))
-        )
-
-    edges = []
-    for d in range(HALO):
-        edges += [lon - 1 - d, d]
-    for i in edges:
-        start_col(i)
+    first = lax.broadcasted_iota(jnp.int32, (lat, lat), 0)
+    second = lax.broadcasted_iota(jnp.int32, (lat, lat), 1)
+
+    def latitude(place):
+        return tiles * (place & (LANES - 1)) + (place >> (LANES.bit_length() - 1))
+
+    to_inner[...] = jnp.where(first == latitude(second), 1.0, 0.0).astype(jnp.bfloat16)
+    to_outer[...] = jnp.where(second == latitude(first), 1.0, 0.0).astype(jnp.bfloat16)
+
+    def permuted(blocks, order):
+        stacked = jnp.concatenate(blocks, axis=0)
+        height = stacked.shape[0]
+        moved = jnp.dot(
+            jnp.concatenate(split_bf16(stacked), axis=0), order[...],
+            preferred_element_type=jnp.float32,
+        )
+        return moved[:height] + moved[height:]
+
+    def tile(value, t):
+        return value[:, t * LANES : (t + 1) * LANES]
+
     wait_loads(2)
-    for i in edges:
-        wind_col(i)
+
+    def load_pair(d, carry):
+        pair = (lon - 1 - d, d)
+        blocks = []
+        for i in pair:
+            scale = column(prior_v, 0, i)
+            for k in range(probe_count):
+                blocks.append(scale * column(probes_v, k * per_probe, i))
+            blocks += [column(wind_v, c * per_probe, i) for c in range(3)]
+        inner = permuted(blocks, to_inner)
+        level = lax.broadcasted_iota(jnp.int32, (LEV, LANES), 0)
+        lane = lax.broadcasted_iota(jnp.int32, (LEV, LANES), 1)
+        for at, i in enumerate(pair):
+            base = at * (rows + 3 * LEV)
+            for t in range(tiles):
+                part = tile(inner[base : base + rows + 3 * LEV], t)
+                fwd[0][HALO + i, t] = part[:rows]
+                east[HALO + i, t] = 0.3 * part[rows : rows + LEV]
+                north = 0.15 * part[rows + LEV : rows + 2 * LEV]
+                north_mix[HALO + i, 0, t] = jnp.where(lane == 0, 0.0, north) if t == 0 else north
+                north_mix[HALO + i, 1, t] = jnp.where(
+                    level == 0, 0.0, 0.025 * (1.0 + part[rows + 2 * LEV :])
+                )
+        return carry
+
+    lax.fori_loop(0, HALO, load_pair, 0)
 
     pl.semaphore_wait(barrier, n - 1)
 
@@ -133,7 +156,7 @@
 
     lax.fori_loop(1, n, send_row, 0)
 
-    arrays = (fwd.at[0], east, north_mix)
+    arrays = (fwd[0], east, north_mix)
 
     def column_copy(kind, side, d):
         if side == 0:
@@ -157,42 +180,79 @@
                 sends.append(column_copy(kind, side, d))
                 sends[-1].start()
 
+    def shifted_levels(ref, s, e, t, k, center):
+        if k > 0:
+            below = ref[s][e, t, pl.ds(k * LEV - 1, LEV), :]
+        else:
+            below = pltpu.roll(center, 1, 0)
+        if k < probe_count - 1:
+            above = ref[s][e, t, pl.ds(k * LEV + 1, LEV), :]
+        else:
+            above = pltpu.roll(center, LEV - 1, 0)
+        return below, above
+
+    def mixed(ref, s, e, t, k, center, mixing, mixing_above):
+        below, above = shifted_levels(ref, s, e, t, k, center)
+        return mixing * (below - center) - mixing_above * (center - above)
+
     def forward_col(s, e):
-        east_here = east[e]
-        east_next = east[e + 1]
-        north = north_mix[e, 0]
-        mixing = north_mix[e, 1]
-        for k in range(probe_count):
-            part = pl.ds(k * LEV, LEV)
-            center = fwd[s, e, part, :]
-            flux = east_here * jnp.where(east_here > 0.0, fwd[s, e - 1, part, :], center)
-            flux_next = east_next * jnp.where(east_next > 0.0, center, fwd[s, e + 1, part, :])
-            south = north * jnp.where(north > 0.0, pltpu.roll(center, 1, 1), center)
-            up = mixing * (pltpu.roll(center, 1, 0) - center)
-            fwd[s + 1, e, part, :] = (
-                center - (flux_next - flux) - (pltpu.roll(south, lat - 1, 1) - south)
-                + (up - pltpu.roll(up, LEV - 1, 0))
-            )
+        for t in range(tiles):
+            east_here = east[e, t]
+            east_next = east[e + 1, t]
+            north = north_mix[e, 0, t]
+            after = (t + 1) % tiles
+            north_after = north_mix[e, 0, after]
+            if t == tiles - 1:
+                north_after = pltpu.roll(north_after, LANES - 1, 1)
+            mixing = north_mix[e, 1, t]
+            mixing_above = pltpu.roll(mixing, LEV - 1, 0)
+            for k in range(probe_count):
+                part = pl.ds(k * LEV, LEV)
+                center = fwd[s][e, t, part, :]
+                flux = east_here * jnp.where(east_here > 0.0, fwd[s][e - 1, t, part, :], center)
+                flux_next = east_next * jnp.where(
+                    east_next > 0.0, center, fwd[s][e + 1, t, part, :]
+                )
+                before = fwd[s][e, (t - 1) % tiles, part, :]
+                if t == 0:
+                    before = pltpu.roll(before, 1, 1)
+                south = north * jnp.where(north > 0.0, before, center)
+                behind = fwd[s][e, after, part, :]
+                if t == tiles - 1:
+                    behind = pltpu.roll(behind, LANES - 1, 1)
+                south_next = north_after * jnp.where(north_after > 0.0, center, behind)
+                fwd[s + 1][e, t, part, :] = (
+                    center - (flux_next - flux) - (south_next - south)
+                    + mixed(fwd, s, e, t, k, center, mixing, mixing_above)
+                )
 
     def backward_col(s, e):
-        east_neg = jnp.minimum(east[e], 0.0)
-        east_pos = jnp.maximum(east[e + 1], 0.0)
-        north = north_mix[e, 0]
-        mixing = north_mix[e, 1]
-        north_pos = jnp.maximum(north, 0.0)
-        north_neg = jnp.minimum(north, 0.0)
-        for k in range(probe_count):
-            part = pl.ds(k * LEV, LEV)
-            center = adj[s, e, part, :]
-            diff = center - pltpu.roll(center, 1, 1)
-            up = mixing * (pltpu.roll(center, 1, 0) - center)
-            adj[s + 1, e, part, :] = (
-                center
-                + east_pos * (adj[s, e + 1, part, :] - center)
-                + east_neg * (center - adj[s, e - 1, part, :])
-                + pltpu.roll(north_pos * diff, lat - 1, 1) + north_neg * diff
-                + (up - pltpu.roll(up, LEV - 1, 0))
-            )
+        for t in range(tiles):
+            east_neg = jnp.minimum(east[e, t], 0.0)
+            east_pos = jnp.maximum(east[e + 1, t], 0.0)
+            after = (t + 1) % tiles
+            north_neg = jnp.minimum(north_mix[e, 0, t], 0.0)
+            north_after = jnp.maximum(north_mix[e, 0, after], 0.0)
+            if t == tiles - 1:
+                north_after = pltpu.roll(north_after, LANES - 1, 1)
+            mixing = north_mix[e, 1, t]
+            mixing_above = pltpu.roll(mixing, LEV - 1, 0)
+            for k in range(probe_count):
+                part = pl.ds(k * LEV, LEV)
+                center = adj[s][e, t, part, :]
+                before = adj[s][e, (t - 1) % tiles, part, :]
+                if t == 0:
+                    before = pltpu.roll(before, 1, 1)
+                behind = adj[s][e, after, part, :]
+                if t == tiles - 1:
+                    behind = pltpu.roll(behind, LANES - 1, 1)
+                adj[s + 1][e, t, part, :] = (
+                    center
+                    + east_pos * (adj[s][e + 1, t, part, :] - center)
+                    + east_neg * (center - adj[s][e - 1, t, part, :])
+                    + north_after * (behind - center) + north_neg * (center - before)
+                    + mixed(adj, s, e, t, k, center, mixing, mixing_above)
+                )
 
     def interior(col):
         for s in range(STEPS - 1):
@@ -203,16 +263,10 @@
             lax.fori_loop(s + 1, lon - 1 - s, body, 0)
 
     def diagonal(col, d):
-        def body(s, carry):
+        for s in range(STEPS):
             col(s, HALO - d + s)
             col(s, HALO + lon - 1 + d - s)
-            return carry
-
-        lax.fori_loop(0, STEPS, body, 0)
-
-    for i in range(HALO, lon - HALO):
-        start_col(i)
-        wind_col(i)
+
     interior(forward_col)
 
     row_recv[me] = row_send[me]
@@ -242,9 +296,9 @@
         return jnp.sum(jnp.where(held, wide, 0.0), axis=0, keepdims=True)
 
     for level in range(LEV):
-        tile = level * CAP // LANES
+        at = level * CAP // LANES
         slots[0, level : level + 1, :] = spread(
-            rows_2d[:, tile * LANES : (tile + 1) * LANES], level * CAP % LANES
+            rows_2d[:, at * LANES : (at + 1) * LANES], level * CAP % LANES
         )
     weight_row = spread(rows_2d[:, LEV * CAP :], 0)
     slots[0, LEV : LEV + 1, :] = spread(tile_column[...].astype(jnp.float32), 0)
@@ -268,7 +322,7 @@
     def make_one_hot(which):
         column, _ = columns_of(which)
         row = jnp.where(column < 0, -1, column & (lat - 1))
-        place = lax.broadcasted_iota(jnp.int32, (lat, total), 0)
+        place = latitude(lax.broadcasted_iota(jnp.int32, (lat, total), 0))
         one_hot[which] = jnp.where(place == row, 1.0, 0.0).astype(jnp.bfloat16)
 
     make_one_hot(0)
@@ -286,7 +340,7 @@
     def forward_diagonal(d, carry):
         for side in range(2):
             pltpu.make_async_remote_copy(
-                src_ref=fwd.at[0, 0], dst_ref=fwd.at[0, 0],
+                src_ref=fwd[0].at[0], dst_ref=fwd[0].at[0],
                 send_sem=col_send.at[0, side, d - 1], recv_sem=col_recv.at[0, side, d - 1],
                 device_id=(group, east_nbr), device_id_type=MESH,
             ).wait_recv()
@@ -310,7 +364,9 @@
         pair = (HALO - d, lon - 1 - HALO + d)
         parts = []
         for i in pair:
-            parts += split_bf16(fwd[STEPS, HALO + i])
+            parts += split_bf16(
+                jnp.concatenate([fwd[STEPS][HALO + i, t] for t in range(tiles)], axis=1)
+            )
         found = jnp.dot(
             jnp.concatenate(parts, axis=0), one_hot[0], preferred_element_type=jnp.float32
         )
@@ -359,9 +415,9 @@
             )
             for q in range(2):
                 base = 2 * rows * q
-                adj[0, first_ext + 2 * p + q] = (
-                    summed[base : base + rows] + summed[base + rows : base + 2 * rows]
-                )
+                both = summed[base : base + rows] + summed[base + rows : base + 2 * rows]
+                for t in range(tiles):
+                    adj[0][first_ext + 2 * p + q, t] = tile(both, t)
             return carry
 
         lax.fori_loop(0, count // 2, body, 0)
@@ -412,18 +468,24 @@
 
     def backward_diagonal(d, carry):
         diagonal(backward_col, d - 1)
-        for i in (HALO - d, lon - 1 - HALO + d):
+        pair = (HALO - d, lon - 1 - HALO + d)
+        pulled = permuted(
+            [
+                jnp.concatenate([adj[STEPS][HALO + i, t] for t in range(tiles)], axis=1)
+                for i in pair
+            ],
+            to_outer,
+        )
+        for at, i in enumerate(pair):
             scale = column(prior_v, 0, i)
             lowest = []
             for k in range(probe_count):
                 value = (
                     column(probes_v, k * per_probe, i)
-                    + scale * adj[STEPS, HALO + i, k * LEV : (k + 1) * LEV, :]
+                    + scale * pulled[at * rows + k * LEV : at * rows + (k + 1) * LEV]
                 )
-                for t in range(lat // LANES):
-                    hess_v[t, pl.ds(k * per_probe + i, LEV, stride=lon), :] = (
-                        value[:, t * LANES : (t + 1) * LANES]
-                    )
+                for t in range(tiles):
+                    hess_v[t, pl.ds(k * per_probe + i, LEV, stride=lon), :] = tile(value, t)
                 lowest.append(value[0:1])
             surface = jnp.concatenate(lowest, axis=0)
             high = surface.astype(jnp.bfloat16).astype(jnp.float32)
@@ -443,7 +505,7 @@
         pltpu.make_async_copy(
             hess_v.at[t], hess_out.at[:, pl.ds(t * LANES, LANES)], load_sem.at[4, t]
         )
-        for t in range(lat // LANES)
+        for t in range(tiles)
     ]
 
     def proj_copy(target, source_id):
@@ -502,6 +564,12 @@
     )
     values = eigen_values[...]
     coeffs_out[...] = values / (1.0 + values) * summed[0:probe_count]
+
+
+def finish_kernel(hess, misfit, coeffs, hess_out, misfit_out, coeffs_out):
+    hess_out[...] = hess[...]
+    misfit_out[...] = misfit[...]
+    coeffs_out[...] = coeffs[...]
 
 
 def local(
@@ -534,10 +602,12 @@
             pltpu.VMEM((lon, lat, rank), f32),
             pltpu.VMEM((lon, lat, 2 * rank), jnp.bfloat16),
             pltpu.VMEM((tiles, rows * lon, LANES), f32),
-            pltpu.VMEM((STEPS + 1, ext, rows, lat), f32),
-            pltpu.VMEM((STEPS + 1, ext, rows, lat), f32),
-            pltpu.VMEM((ext, LEV, lat), f32),
-            pltpu.VMEM((ext, 2, LEV, lat), f32),
+            pltpu.VMEM((lat, lat), jnp.bfloat16),
+            pltpu.VMEM((lat, lat), jnp.bfloat16),
+            (pltpu.VMEM((ext, tiles, rows, LANES), f32),) * (STEPS + 1),
+            (pltpu.VMEM((ext, tiles, rows, LANES), f32),) * (STEPS + 1),
+            pltpu.VMEM((ext, tiles, LEV, LANES), f32),
+            pltpu.VMEM((ext, 2, tiles, LEV, LANES), f32),
             pltpu.VMEM((n, 1, LEV * CAP + LANES), f32),
             pltpu.VMEM((n, 1, LEV * CAP + LANES), f32),
             pltpu.VMEM((n, LEV * CAP + LANES), f32),
@@ -577,6 +647,12 @@
         obs_weight,
         tile_column,
     )
+    hess, misfit, coeffs = pl.pallas_call(
+        finish_kernel,
+        out_shape=tuple(jax.ShapeDtypeStruct(x.shape, f32) for x in (hess, misfit, coeffs)),
+        in_specs=[vmem] * 3,
+        out_specs=(vmem,) * 3,
+    )(hess, misfit, coeffs)
     return hess.reshape(probes.shape), misfit, coeffs
 
 

time: 53 us -> 48.3 us (0.911)
  local copies, waits for them, and re-layouts: 3.45 us -> 0 us
  Pallas kernels: 48.6 us -> 47.4 us
    pallas_call x1, Pallas kernels: 48.6 us -> 45.1 us  [local(): pl.pallas_call(kernel, out_shape=(jax.ShapeDtypeStruct((rows * lon, lat),...]
    unnamed x7 -> x0, local copies, waits for them, and re-layouts: 3.45 us -> none
    pallas_call x0 -> x1, Pallas kernels: none -> 2.29 us  [local(): pl.pallas_call(finish_kernel, out_shape=tuple((jax.ShapeDtypeStruct(x.sha...]
where the time goes in v2:
time: 48.3 us; the launch traced here: 48.1 us
  Pallas kernels  47.4 us (98%)
  between operations  0.64 us (1%)
    pallas_call x1, Pallas kernels, local(): pl.pallas_call(kernel, out_shape=(jax.ShapeDtypeStruct((rows * lon, lat),...  45.1 us
    pallas_call x1, Pallas kernels, local(): pl.pallas_call(finish_kernel, out_shape=tuple((jax.ShapeDtypeStruct(x.sha...  2.29 us

profile of v2, /device:TPU:0, one launch (start us, length us, event | category | flops | bytes accessed | tf_op | source)
XLA Modules:
  0.0 48.1 jit_solution(10645733785639354458)
XLA Ops:
  0.6 45.1 %shard_map.103 = (f32[512,512]{1,0:T(8,128)}, f32[16,128]{1,0:T(8,128)}, f32[4,128]{1,0:T(4,128)}) custom-call(f32[512,512]{1,0:T(8,128)} %bitcast.5, f32[384,512]{1,0:T(8,128)} %bitcast.6, f32[128,512]{1,0:T(8,128)} %bitcast.7, f32[8,512,128]{2,1,0:T(8,128)} %basis.1, f32[1,128]{1,0:T(1,128)} %bitcast.8, f32[16,512]{1,0:T(8,128)} %kernel_rows.1, ...), custom_call_target="tpu_custom_call" | custom-call | tf_op jit(solution)/shard_map/pallas_call | solution.py:589
  45.8 2.3 %shard_map.104 = (f32[512,512]{1,0:T(8,128)}, f32[16,128]{1,0:T(8,128)}, f32[4,128]{1,0:T(4,128)}) custom-call(f32[512,512]{1,0:T(8,128)} %get-tuple-element.9.hess, f32[16,128]{1,0:T(8,128)} %get-tuple-element.10.misfit, f32[4,128]{1,0:T(4,128)} %get-tuple-element.11.coeffs), custom_call_target="tpu_custom_call" | custom-call | tf_op jit(solution)/shard_map/pallas_call | solution.py:650

commit v3 on v2

--- a/solution.py
+++ b/solution.py
@@ -25,15 +25,16 @@
 def kernel(
     probes, wind, prior, basis, eigen_values, kernel_rows, obs_weight, tile_column,
     hess_out, misfit_out, coeffs_out,
-    probes_v, wind_v, prior_v, basis_v, basis_split, hess_v, to_inner, to_outer,
-    fwd, adj, east, north_mix, row_send, row_recv, rows_2d, slots, weighted, one_hot, sampled,
+    probes_v, wind_v, prior_v, basis_v, basis_split, hess_v, to_inner, to_outer, surface,
+    fwd, adj, rates, row_send, row_recv, rows_2d, slots, weighted, one_hot, sampled,
     mis_2d, mis_send, mis_recv, proj, proj_recv,
     load_sem, col_send, col_recv, row_ssem, row_rsem, slot_ssem, slot_rsem, wt_ssem, wt_rsem,
-    mis_ssem, mis_rsem, proj_ssem, proj_rsem,
+    mis_ssem, mis_rsem, proj_ssem, proj_rsem, hand_ssem, hand_rsem,
 ):
     group = lax.axis_index("groups")
     me = lax.axis_index("cells")
     n = lax.axis_size("cells")
+    group_count = lax.axis_size("groups")
     east_nbr = lax.rem(me + 1, n)
     west_nbr = lax.rem(me + n - 1, n)
     lat = probes.shape[1]
@@ -53,6 +54,10 @@
         return carry
 
     lax.fori_loop(1, n, greet, 0)
+    for o in range(1, group_count):
+        pl.semaphore_signal(
+            barrier, inc=1, device_id=(lax.rem(group + o, group_count), me), device_id_type=MESH
+        )
 
     def tile_loads(source, target, at):
         return [
@@ -131,17 +136,17 @@
             for t in range(tiles):
                 part = tile(inner[base : base + rows + 3 * LEV], t)
                 fwd[0][HALO + i, t] = part[:rows]
-                east[HALO + i, t] = 0.3 * part[rows : rows + LEV]
+                rates[HALO + i, t, 0] = 0.3 * part[rows : rows + LEV]
                 north = 0.15 * part[rows + LEV : rows + 2 * LEV]
-                north_mix[HALO + i, 0, t] = jnp.where(lane == 0, 0.0, north) if t == 0 else north
-                north_mix[HALO + i, 1, t] = jnp.where(
+                rates[HALO + i, t, 1] = jnp.where(lane == 0, 0.0, north) if t == 0 else north
+                rates[HALO + i, t, 2] = jnp.where(
                     level == 0, 0.0, 0.025 * (1.0 + part[rows + 2 * LEV :])
                 )
         return carry
 
     lax.fori_loop(0, HALO, load_pair, 0)
 
-    pl.semaphore_wait(barrier, n - 1)
+    pl.semaphore_wait(barrier, n - 1 + group_count - 1)
 
     def row_copy(target, source_id):
         return pltpu.make_async_remote_copy(
@@ -156,28 +161,60 @@
 
     lax.fori_loop(1, n, send_row, 0)
 
-    arrays = (fwd[0], east, north_mix)
-
-    def column_copy(kind, side, d):
+    share = tiles // group_count
+
+    def places(side, d):
         if side == 0:
-            source, target, device = HALO + lon - 1 - d, HALO - 1 - d, east_nbr
-        else:
-            source, target, device = HALO + d, HALO + lon + d, west_nbr
+            return HALO + lon - 1 - d, HALO - 1 - d, east_nbr
+        return HALO + d, HALO + lon + d, west_nbr
+
+    def rate_part(e, d, owner):
+        if d < HALO - 1:
+            return rates.at[e, pl.ds(owner * share, share)]
+        return rates.at[e, pl.ds(owner * share, share), 0]
+
+    def tracer_copy(side, d):
+        source, target, device = places(side, d)
         return pltpu.make_async_remote_copy(
-            src_ref=arrays[kind].at[source], dst_ref=arrays[kind].at[target],
-            send_sem=col_send.at[kind, side, d], recv_sem=col_recv.at[kind, side, d],
+            src_ref=fwd[0].at[source], dst_ref=fwd[0].at[target],
+            send_sem=col_send.at[0, side, d], recv_sem=col_recv.at[0, side, d],
             device_id=(group, device), device_id_type=MESH,
         )
 
+    def rate_copy(side, d):
+        source, target, device = places(side, d)
+        return pltpu.make_async_remote_copy(
+            src_ref=rate_part(source, d, group), dst_ref=rate_part(target, d, group),
+            send_sem=col_send.at[1, side, d], recv_sem=col_recv.at[1, side, d],
+            device_id=(group, device), device_id_type=MESH,
+        )
+
     sends = []
+    rate_plan = [(side, d) for d in range(HALO) for side in range(2) if d < HALO - 1 or side == 1]
+    for side, d in rate_plan:
+        sends.append(rate_copy(side, d))
+        sends[-1].start()
     for d in range(HALO):
-        for kind in range(3):
-            if kind == 2 and d == HALO - 1:
+        for side in range(2):
+            sends.append(tracer_copy(side, d))
+            sends[-1].start()
+
+    def hand_on(at):
+        for side, d in rate_plan:
+            if d != at:
                 continue
-            for side in range(2):
-                if kind == 1 and d == HALO - 1 and side == 0:
-                    continue
-                sends.append(column_copy(kind, side, d))
+            rate_copy(side, d).wait_recv()
+            part = rate_part(places(side, d)[1], d, group)
+            for o in range(1, group_count):
+                peer = lax.rem(group + o, group_count)
+                sends.append(
+                    pltpu.make_async_remote_copy(
+                        src_ref=part, dst_ref=part,
+                        send_sem=hand_ssem.at[side, d, peer],
+                        recv_sem=hand_rsem.at[side, d, group],
+                        device_id=(peer, me), device_id_type=MESH,
+                    )
+                )
                 sends[-1].start()
 
     def shifted_levels(ref, s, e, t, k, center):
@@ -197,14 +234,14 @@
 
     def forward_col(s, e):
         for t in range(tiles):
-            east_here = east[e, t]
-            east_next = east[e + 1, t]
-            north = north_mix[e, 0, t]
+            east_here = rates[e, t, 0]
+            east_next = rates[e + 1, t, 0]
+            north = rates[e, t, 1]
             after = (t + 1) % tiles
-            north_after = north_mix[e, 0, after]
+            north_after = rates[e, after, 1]
             if t == tiles - 1:
                 north_after = pltpu.roll(north_after, LANES - 1, 1)
-            mixing = north_mix[e, 1, t]
+            mixing = rates[e, t, 2]
             mixing_above = pltpu.roll(mixing, LEV - 1, 0)
             for k in range(probe_count):
                 part = pl.ds(k * LEV, LEV)
@@ -228,14 +265,14 @@
 
     def backward_col(s, e):
         for t in range(tiles):
-            east_neg = jnp.minimum(east[e, t], 0.0)
-            east_pos = jnp.maximum(east[e + 1, t], 0.0)
+            east_neg = jnp.minimum(rates[e, t, 0], 0.0)
+            east_pos = jnp.maximum(rates[e + 1, t, 0], 0.0)
             after = (t + 1) % tiles
-            north_neg = jnp.minimum(north_mix[e, 0, t], 0.0)
-            north_after = jnp.maximum(north_mix[e, 0, after], 0.0)
+            north_neg = jnp.minimum(rates[e, t, 1], 0.0)
+            north_after = jnp.maximum(rates[e, after, 1], 0.0)
             if t == tiles - 1:
                 north_after = pltpu.roll(north_after, LANES - 1, 1)
-            mixing = north_mix[e, 1, t]
+            mixing = rates[e, t, 2]
             mixing_above = pltpu.roll(mixing, LEV - 1, 0)
             for k in range(probe_count):
                 part = pl.ds(k * LEV, LEV)
@@ -297,6 +334,8 @@
 
     for level in range(LEV):
         at = level * CAP // LANES
+        if level % 4 == 0:
+            hand_on(level // 4)
         slots[0, level : level + 1, :] = spread(
             rows_2d[:, at * LANES : (at + 1) * LANES], level * CAP % LANES
         )
@@ -338,27 +377,25 @@
     lax.fori_loop(0, lon, split_basis, 0)
 
     def forward_diagonal(d, carry):
-        for side in range(2):
+        def wait_for(ref, recv_sem):
             pltpu.make_async_remote_copy(
-                src_ref=fwd[0].at[0], dst_ref=fwd[0].at[0],
-                send_sem=col_send.at[0, side, d - 1], recv_sem=col_recv.at[0, side, d - 1],
+                src_ref=ref, dst_ref=ref, send_sem=col_send.at[0, 0, 0], recv_sem=recv_sem,
                 device_id=(group, east_nbr), device_id_type=MESH,
             ).wait_recv()
 
-        def wait_wind(kind, side, at):
-            pltpu.make_async_remote_copy(
-                src_ref=arrays[kind].at[0], dst_ref=arrays[kind].at[0],
-                send_sem=col_send.at[kind, side, at], recv_sem=col_recv.at[kind, side, at],
-                device_id=(group, east_nbr), device_id_type=MESH,
-            ).wait_recv()
-
-        wait_wind(1, 1, d - 1)
-
-        @pl.when(d > 1)
-        def _():
-            wait_wind(1, 0, d - 2)
-            wait_wind(2, 0, d - 2)
-            wait_wind(2, 1, d - 2)
+        for side in range(2):
+            wait_for(fwd[0].at[0], col_recv.at[0, side, d - 1])
+        for o in range(1, group_count):
+            peer = lax.rem(group + o, group_count)
+
+            @pl.when(d < HALO)
+            def _():
+                for side in range(2):
+                    wait_for(rates.at[0, pl.ds(0, share)], hand_rsem.at[side, d - 1, peer])
+
+            @pl.when(d == HALO)
+            def _():
+                wait_for(rates.at[0, pl.ds(0, share), 0], hand_rsem.at[1, d - 1, peer])
 
         diagonal(forward_col, d - 1)
         pair = (HALO - d, lon - 1 - HALO + d)
@@ -464,11 +501,66 @@
     inject(1, lon - HALO, 0, HALO)
     inject(2, 0, HALO + lon, HALO)
 
-    proj[...] = jnp.zeros_like(proj)
-
     def backward_diagonal(d, carry):
         diagonal(backward_col, d - 1)
-        pair = (HALO - d, lon - 1 - HALO + d)
+        return carry
+
+    lax.fori_loop(1, HALO + 1, backward_diagonal, 0)
+
+    for k in range(probe_count):
+        for i in range(lon):
+            for t in range(tiles):
+                surface[k * lon + i : k * lon + i + 1, t * LANES : (t + 1) * LANES] = (
+                    adj[STEPS][HALO + i, t, k * LEV : k * LEV + 1, :]
+                )
+    pulled_low = permuted([surface[...]], to_outer)
+
+    def lowest(ref, base):
+        return jnp.concatenate([ref[t, base : base + lon, :] for t in range(tiles)], axis=1)
+
+    low = jnp.concatenate(
+        [
+            lowest(probes_v, k * per_probe)
+            + lowest(prior_v, 0) * pulled_low[k * lon : (k + 1) * lon]
+            for k in range(probe_count)
+        ],
+        axis=0,
+    )
+    height = probe_count * lon
+    split_low = jnp.concatenate(split_bf16(low), axis=0)
+    own_lon = lax.broadcasted_iota(jnp.int32, (height, LANES), 0) & (lon - 1)
+    total_low = jnp.zeros((height, LANES), jnp.float32)
+    for i in range(lon):
+        out = jnp.dot(split_low, basis_split[i], preferred_element_type=jnp.float32)
+        part = out[:height, :LANES] + (out[:height, LANES:] + out[height:, :LANES])
+        total_low = total_low + jnp.where(own_lon == i, part, 0.0)
+    proj[...] = jnp.zeros_like(proj)
+    for k in range(probe_count):
+        proj[k : k + 1, :] = jnp.sum(total_low[k * lon : (k + 1) * lon], axis=0, keepdims=True)
+
+    stores = [
+        pltpu.make_async_copy(
+            hess_v.at[t], hess_out.at[:, pl.ds(t * LANES, LANES)], load_sem.at[4, t]
+        )
+        for t in range(tiles)
+    ]
+
+    def proj_copy(target, source_id):
+        return pltpu.make_async_remote_copy(
+            src_ref=proj, dst_ref=proj_recv.at[source_id],
+            send_sem=proj_ssem.at[target], recv_sem=proj_rsem.at[source_id],
+            device_id=(group, target), device_id_type=MESH,
+        )
+
+    def send_proj(i, carry):
+        proj_copy(lax.rem(me + i, n), me).start()
+        return carry
+
+    lax.fori_loop(1, n, send_proj, 0)
+    proj_recv[me] = proj[...]
+
+    def finish_pair(d, carry):
+        pair = (d, lon - 1 - d)
         pulled = permuted(
             [
                 jnp.concatenate([adj[STEPS][HALO + i, t] for t in range(tiles)], axis=1)
@@ -478,7 +570,6 @@
         )
         for at, i in enumerate(pair):
             scale = column(prior_v, 0, i)
-            lowest = []
             for k in range(probe_count):
                 value = (
                     column(probes_v, k * per_probe, i)
@@ -486,43 +577,11 @@
                 )
                 for t in range(tiles):
                     hess_v[t, pl.ds(k * per_probe + i, LEV, stride=lon), :] = tile(value, t)
-                lowest.append(value[0:1])
-            surface = jnp.concatenate(lowest, axis=0)
-            high = surface.astype(jnp.bfloat16).astype(jnp.float32)
-            stacked = jnp.concatenate(
-                [high, surface - high, jnp.zeros((16 - 2 * probe_count, lat), jnp.float32)], axis=0
-            ).astype(jnp.bfloat16)
-            out = jnp.dot(stacked, basis_split[i], preferred_element_type=jnp.float32)
-            proj[0:probe_count, :] = proj[0:probe_count, :] + (
-                out[0:probe_count, 0:LANES]
-                + (out[0:probe_count, LANES:] + out[probe_count : 2 * probe_count, 0:LANES])
-            )
-        return carry
-
-    lax.fori_loop(1, HALO + 1, backward_diagonal, 0)
-
-    stores = [
-        pltpu.make_async_copy(
-            hess_v.at[t], hess_out.at[:, pl.ds(t * LANES, LANES)], load_sem.at[4, t]
-        )
-        for t in range(tiles)
-    ]
-
-    def proj_copy(target, source_id):
-        return pltpu.make_async_remote_copy(
-            src_ref=proj, dst_ref=proj_recv.at[source_id],
-            send_sem=proj_ssem.at[target], recv_sem=proj_rsem.at[source_id],
-            device_id=(group, target), device_id_type=MESH,
-        )
-
-    def send_proj(i, carry):
-        proj_copy(lax.rem(me + i, n), me).start()
-        return carry
-
-    lax.fori_loop(1, n, send_proj, 0)
+        return carry
+
+    lax.fori_loop(0, HALO, finish_pair, 0)
     for store in stores:
         store.start()
-    proj_recv[me] = proj[...]
 
     mis_recv[me] = mis_send[me]
 
@@ -604,10 +663,10 @@
             pltpu.VMEM((tiles, rows * lon, LANES), f32),
             pltpu.VMEM((lat, lat), jnp.bfloat16),
             pltpu.VMEM((lat, lat), jnp.bfloat16),
+            pltpu.VMEM((probe_count * lon, lat), f32),
             (pltpu.VMEM((ext, tiles, rows, LANES), f32),) * (STEPS + 1),
             (pltpu.VMEM((ext, tiles, rows, LANES), f32),) * (STEPS + 1),
-            pltpu.VMEM((ext, tiles, LEV, LANES), f32),
-            pltpu.VMEM((ext, 2, tiles, LEV, LANES), f32),
+            pltpu.VMEM((ext, tiles, 3, LEV, LANES), f32),
             pltpu.VMEM((n, 1, LEV * CAP + LANES), f32),
             pltpu.VMEM((n, 1, LEV * CAP + LANES), f32),
             pltpu.VMEM((n, LEV * CAP + LANES), f32),
@@ -621,8 +680,8 @@
             pltpu.VMEM((8, rank), f32),
             pltpu.VMEM((n, 8, rank), f32),
             dma((5, tiles)),
-            dma((3, 2, HALO)),
-            dma((3, 2, HALO)),
+            dma((2, 2, HALO)),
+            dma((2, 2, HALO)),
             dma((n,)),
             dma((n,)),
             dma((2,)),
@@ -633,6 +692,8 @@
             dma((n,)),
             dma((n,)),
             dma((n,)),
+            dma((2, HALO, lax.axis_size("groups"))),
+            dma((2, HALO, lax.axis_size("groups"))),
         ],
         compiler_params=pltpu.CompilerParams(
             collective_id=1, has_side_effects=True, vmem_limit_bytes=56 * 1024 * 1024

time: 48.3 us -> 43.6 us (0.903)
  Pallas kernels: 47.4 us -> 42.8 us
    pallas_call x1, Pallas kernels: 45.1 us -> 40.5 us  [local(): pl.pallas_call(kernel, out_shape=(jax.ShapeDtypeStruct((rows * lon, lat),...]
where the time goes in v3:
time: 43.6 us; the launch traced here: 43.4 us
  Pallas kernels  42.8 us (98%)
  between operations  0.64 us (1%)
    pallas_call x1, Pallas kernels, local(): pl.pallas_call(kernel, out_shape=(jax.ShapeDtypeStruct((rows * lon, lat),...  40.5 us
    pallas_call x1, Pallas kernels, local(): pl.pallas_call(finish_kernel, out_shape=tuple((jax.ShapeDtypeStruct(x.sha...  2.29 us

profile of v3, /device:TPU:0, one launch (start us, length us, event | category | flops | bytes accessed | tf_op | source)
XLA Modules:
  0.0 43.4 jit_solution(5014219651360559754)
XLA Ops:
  0.6 40.5 %shard_map.103 = (f32[512,512]{1,0:T(8,128)}, f32[16,128]{1,0:T(8,128)}, f32[4,128]{1,0:T(4,128)}) custom-call(f32[512,512]{1,0:T(8,128)} %bitcast.5, f32[384,512]{1,0:T(8,128)} %bitcast.6, f32[128,512]{1,0:T(8,128)} %bitcast.7, f32[8,512,128]{2,1,0:T(8,128)} %basis.1, f32[1,128]{1,0:T(1,128)} %bitcast.8, f32[16,512]{1,0:T(8,128)} %kernel_rows.1, ...), custom_call_target="tpu_custom_call" | custom-call | tf_op jit(solution)/shard_map/pallas_call | solution.py:648
  41.1 2.3 %shard_map.104 = (f32[512,512]{1,0:T(8,128)}, f32[16,128]{1,0:T(8,128)}, f32[4,128]{1,0:T(4,128)}) custom-call(f32[512,512]{1,0:T(8,128)} %get-tuple-element.9.hess, f32[16,128]{1,0:T(8,128)} %get-tuple-element.10.misfit, f32[4,128]{1,0:T(4,128)} %get-tuple-element.11.coeffs), custom_call_target="tpu_custom_call" | custom-call | tf_op jit(solution)/shard_map/pallas_call | solution.py:711
